TPU v7x, 32 devices: a whole 2x2x4 slice. The times are simulated.
32 devices in a mesh: rep: 2 (over x), section: 2 (over core), tp: 8 (over z, y).
Axes of the slice: x: 2, y: 2, z: 4, core: 2. Of those that a mesh axis runs over, the one named last changes fastest.
Arguments:
- queries: bfloat16 [2, 16, 64, 128], P('section', 'rep', 'tp'), parts along dimension 1, may hold values from -200 to 200
- new_kv: bfloat16 [2, 16, 2, 4, 128], P('section', 'rep'), parts along dimension 1, may hold values from -6 to 6
- kv_cache: bfloat16 [2, 16, 2, 4, 1024, 128], P('section', 'rep', None, None, 'tp'), parts along dimension 1, may hold values from -6 to 6
- lengths: int32 [2, 16], P('section', 'rep'), parts along dimension 1, may hold values from 2 to 1023, as said below
- residual: bfloat16 [2, 16, 16384], P('section', 'rep', 'tp'), parts along dimension 1, may hold values from -3 to 3
- out_weight: bfloat16 [2, 8192, 16384], P('section', 'tp'), may hold values from -0.09375 to 0.09375
Outputs:
- handed: bfloat16 [2, 16, 16384], P('section', 'rep'), parts along dimension 1
There are 2 independent parts, one for each index of `rep`. A program takes and returns all parts, laid end to end along the dimension named above; an argument that names none is the same for every part. Nothing has to cross between parts.
Inputs may be any that keep to these rules, and one draw needn't show every extreme that they name: Row r attends to cached positions 0 to lengths - 1 and to its new token at position lengths; in each section some row has the largest value.
All inputs are finite; a program needn't handle non-finite values.
Results may differ from a plain program's by a relative error of at most 0.039.
Values may be sent and summed in bfloat16 or wider, within the bound.
No kernel may reach another device: no remote copies, remote signals or barrier semaphores. Data moves between devices by JAX's collectives and lax.ppermute only.
A program may use at most 192 MiB of HBM per device.

v0:
```python
import functools
import math

import jax
import jax.numpy as jnp
from jax import lax
from jax.experimental import pallas as pl
from jax.experimental.pallas import tpu as pltpu
from jax.sharding import PartitionSpec as P

QB = 128
LANES = 128
STAT_ROWS = 16
MIB = 1 << 20
F32 = jnp.float32
BF16 = jnp.bfloat16
VMEM_SPEC = pl.BlockSpec(memory_space=pltpu.VMEM)
ANY_SPEC = pl.BlockSpec(memory_space=pl.ANY)


def pieces(x):
    high = x.astype(BF16).astype(F32)
    rest = x - high
    middle = rest.astype(BF16).astype(F32)
    return high, middle, rest - middle


def weight_copies(slots, weight_ref, held_ref, sems):
    rank = lax.axis_index("tp")
    width = held_ref.shape[2]
    copies = []
    for i, slot in enumerate(slots):
        start = pl.multiple_of((rank ^ slot) * width, width)
        copies.append(
            pltpu.make_async_copy(
                weight_ref.at[0, :, pl.ds(start, width)], held_ref.at[i], sems.at[i]
            )
        )
    return copies


def stage_cache_kernel(
    per, lengths_ref, new_ref, kv_ref, queries_ref, stored_ref, limit_ref, near_ref,
    lengths, new, kv, sems,
):
    rank = lax.axis_index("tp")
    rows, _, kv_heads, span, dim = kv.shape
    copies = [
        pltpu.make_async_copy(lengths_ref, lengths, sems.at[0]),
        pltpu.make_async_copy(new_ref.at[0], new, sems.at[1]),
        pltpu.make_async_copy(kv_ref.at[0], kv, sems.at[2]),
        pltpu.make_async_copy(queries_ref, near_ref, sems.at[3]),
    ]
    for copy in copies:
        copy.start()
    for copy in copies:
        copy.wait()
    first = rank * span
    sub = lax.broadcasted_iota(jnp.int32, (span, dim), 0)
    kv_sub = lax.broadcasted_iota(jnp.int32, (kv_heads, dim), 0)
    row_of = lax.broadcasted_iota(jnp.int32, (rows, span), 0)
    limit = jnp.zeros((rows, span), jnp.int32)
    for r in range(rows):
        limit = jnp.where(row_of == r, lengths[0, r] - first, limit)
        written = sub == lengths[0, r] - first
        for which in range(2):
            new_heads = new[r, which].astype(F32)
            for m in range(kv_heads):
                head = (rank // per) ^ m
                fresh = jnp.sum(
                    jnp.where(kv_sub == head, new_heads, 0.0), axis=0, keepdims=True
                )
                block = kv[r, which, head].astype(F32)
                stored_ref[r, which, m] = jnp.where(written, fresh, block).astype(BF16)
    limit_ref[...] = limit


def stage_kernel(slots, weight_ref, after_ref, held_ref, sems):
    del after_ref
    copies = weight_copies(slots, weight_ref, held_ref, sems)
    for copy in copies:
        copy.start()
    for copy in copies:
        copy.wait()


def append_kernel(first_ref, second_ref, after_ref, out_ref):
    del after_ref
    count = first_ref.shape[0]
    out_ref[:count] = first_ref[...]
    out_ref[count:] = second_ref[...]


def packed(mixed, top, total):
    stat_sub = lax.broadcasted_iota(jnp.int32, (STAT_ROWS, LANES), 0)
    tile = jnp.zeros((STAT_ROWS, LANES), F32)
    for i, piece in enumerate(pieces(top) + pieces(total)):
        tile = jnp.where(stat_sub == i, piece, tile)
    return jnp.concatenate([mixed, tile], axis=0).astype(BF16)


def to_lanes(column):
    n = column.shape[0]
    sub = lax.broadcasted_iota(jnp.int32, (n, LANES), 0)
    lane = lax.broadcasted_iota(jnp.int32, (n, LANES), 1)
    return jnp.sum(jnp.where(lane == sub, column, 0.0), axis=0, keepdims=True)


def to_column(row, n):
    sub = lax.broadcasted_iota(jnp.int32, (n, LANES), 0)
    lane = lax.broadcasted_iota(jnp.int32, (n, LANES), 1)
    return jnp.sum(jnp.where(lane == sub, row, 0.0), axis=1, keepdims=True)


def merged(first, second):
    n = first.shape[0] - STAT_ROWS
    tops, sums = [], []
    for block in (first, second):
        tile = block[n:].astype(F32)
        tops.append(tile[0:1] + tile[1:2] + tile[2:3])
        sums.append(tile[3:4] + tile[4:5] + tile[5:6])
    top = jnp.maximum(*tops)
    factors = [jnp.exp(own - top) for own in tops]
    total = sums[0] * factors[0] + sums[1] * factors[1]
    mixed = first[:n].astype(F32) * to_column(factors[0], n)
    mixed = mixed + second[:n].astype(F32) * to_column(factors[1], n)
    return mixed, top, total


def attention_kernel(
    low_ref, high_ref, stored_ref, limit_ref, after_ref, send_ref, keep_ref, scores_ref, mixed_ref
):
    del after_ref
    half, rows, heads, dim = low_ref.shape
    tp = 2 * half
    bits = tp.bit_length() - 1
    kv_heads, span = stored_ref.shape[2:4]
    group = heads * tp // kv_heads
    per = group // heads
    scale = 1.0 / math.sqrt(dim)

    def query(k, r):
        source = high_ref if k & 1 else low_ref
        at = sum(((k >> b) & 1) << (bits - 1 - b) for b in range(1, bits))
        return source[at, r].astype(F32)

    for m in range(kv_heads):
        for r in range(rows):
            q = jnp.concatenate([query(m * per + i, r) for i in range(per)], axis=0).astype(BF16)
            s = lax.dot_general(
                q, stored_ref[r, 0, m], (((1,), (1,)), ((), ())), preferred_element_type=F32
            )
            scores_ref[m * group : (m + 1) * group, r, :] = s * scale

    pos = lax.broadcasted_iota(jnp.int32, (rows, span), 1)
    visible = (pos <= limit_ref[...])[None]
    scores = jnp.where(visible, scores_ref[...], -1e30)
    top = jnp.max(scores, axis=-1, keepdims=True)
    weights = jnp.where(visible, jnp.exp(scores - top), 0.0)
    total = jnp.sum(weights, axis=-1, keepdims=True)
    scores_ref[...] = weights

    for m in range(kv_heads):
        for r in range(rows):
            w = scores_ref[m * group : (m + 1) * group, r, :].astype(BF16)
            mixed_ref[m * group : (m + 1) * group, r, :] = jnp.dot(
                w, stored_ref[r, 1, m], preferred_element_type=F32
            )

    n = heads * rows
    for k in range(tp):
        own = slice(k * heads, (k + 1) * heads)
        block = packed(
            mixed_ref[own].reshape(n, dim),
            to_lanes(top[own].reshape(n, 1)),
            to_lanes(total[own].reshape(n, 1)),
        )
        if k & 1:
            send_ref[k >> 1] = block
        else:
            keep_ref[k >> 1] = block


def merge_kernel(kept_ref, got_ref, after_ref, send_ref, keep_ref):
    del after_ref
    for i in range(keep_ref.shape[0]):
        keep_ref[i] = packed(*merged(kept_ref[2 * i], got_ref[2 * i]))
        send_ref[i] = packed(*merged(kept_ref[2 * i + 1], got_ref[2 * i + 1]))


def requantized(x):
    top = jnp.max(jnp.abs(x), axis=-1, keepdims=True)
    scale = ((top + 1e-06) / 127.0).astype(BF16).astype(F32)
    return jnp.clip(jnp.floor(x / scale + 0.5), -127.0, 127.0) * scale


def project_slot(flat, weight, out_ref, i):
    width = weight.shape[1]
    tile = min(512, width)
    for c in range(0, width, tile):
        part = jnp.dot(flat, weight[:, c : c + tile], preferred_element_type=F32)
        for b in range(0, tile, QB):
            block = requantized(part[:, b : b + QB])
            out_ref[i, :, c + b : c + b + QB] = block.astype(out_ref.dtype)


def project_away_kernel(
    rows, heads, places, slots, kept_ref, got_ref, weight_ref, *refs
):
    held, (flat_ref, out_ref, next_ref, sems) = refs[:-4], refs[-4:]
    copies = weight_copies(slots, weight_ref, next_ref, sems)
    for copy in copies:
        copy.start()
    mixed, _, total = merged(kept_ref[0], got_ref[0])
    attended = mixed / to_column(total, mixed.shape[0])
    flat = jnp.concatenate(
        [attended[h * rows : (h + 1) * rows] for h in range(heads)], axis=1
    ).astype(BF16)
    flat_ref[...] = flat
    for i, (array, index) in enumerate(places):
        project_slot(flat, held[array].at[index], out_ref, i)
    for copy in copies:
        copy.wait()


def project_own_kernel(places, slots, order, flat_ref, weight_ref, *refs):
    held, (out_ref, late_ref, sems) = refs[:-3], refs[-3:]
    copies = weight_copies(slots, weight_ref, late_ref, sems)
    for copy in copies:
        copy.start()
    flat = flat_ref[...]
    for i in order:
        if places[i] is None:
            continue
        array, index = places[i]
        project_slot(flat, held[array].at[index], out_ref, i)
    for late, slot in enumerate(slots):
        copies[late].wait()
        project_slot(flat, late_ref.at[late], out_ref, slot >> 1)


def split_kernel(kept_ref, got_ref, send_ref, keep_ref):
    for i in range(send_ref.shape[0]):
        send_ref[i] = (kept_ref[2 * i + 1] + got_ref[2 * i + 1].astype(F32)).astype(BF16)
        keep_ref[i] = kept_ref[2 * i] + got_ref[2 * i].astype(F32)


def total_kernel(kept_ref, got_ref, residual_ref, out_ref):
    own = kept_ref[0] + got_ref[0].astype(F32) + residual_ref[0].astype(F32)
    out_ref[0] = own.astype(BF16)
    out_ref[1] = (kept_ref[1] + got_ref[1].astype(F32)).astype(BF16)


def owner_kernel(near_ref, far_ref, out_ref):
    for i in range(2):
        for b in range(0, out_ref.shape[2], QB):
            at = slice(b, b + QB)
            x = near_ref[i, :, at].astype(F32) + far_ref[1 - i, :, at].astype(F32)
            out_ref[i, :, at] = requantized(x).astype(BF16)


def place_kernel(offsets, high, *refs):
    blocks, out_ref = refs[:-1], refs[-1]
    width = blocks[0].shape[2]
    rank = lax.axis_index("tp")
    for offset, block in zip(offsets, blocks):
        for i in range(2):
            start = pl.multiple_of((rank ^ offset ^ (i * high)) * width, width)
            out_ref[0, :, pl.ds(start, width)] = block[i]


def call(kernel, name, outs, args, in_specs=None, scratch=(), mib=4, cost=MIB):
    return pl.pallas_call(
        kernel,
        out_shape=outs,
        in_specs=in_specs or [VMEM_SPEC] * len(args),
        out_specs=jax.tree.map(lambda _: VMEM_SPEC, outs),
        scratch_shapes=scratch,
        compiler_params=pltpu.CompilerParams(vmem_limit_bytes=mib * MIB),
        cost_estimate=pl.CostEstimate(flops=cost, bytes_accessed=cost, transcendentals=0),
        name=name,
    )(*args)


def in_hbm(array):
    return pltpu.with_memory_space_constraint(array, pltpu.HBM)


def local(tp, sections, queries, new_kv, kv_cache, lengths, residual, out_weight):
    rows, heads, dim = queries.shape[1:]
    kv_heads, span = kv_cache.shape[3:5]
    depth, full = out_weight.shape[1:]
    width = full // tp
    half = tp // 2
    bits = tp.bit_length() - 1
    struct = jax.ShapeDtypeStruct

    def exchanged(array, k, shift=0):
        pairs = [
            (s * tp + t, ((s + shift) % sections) * tp + (t ^ k))
            for s in range(sections)
            for t in range(tp)
        ]
        return lax.ppermute(array, ("section", "tp"), pairs)

    weight = in_hbm(out_weight)
    order = list(range(1, tp, 2)) + list(range(0, tp, 2))
    windows = 2 * bits - 1
    each = max(1, tp * 5 // 8 // windows)
    staged = []

    def stage(after):
        slots = order[len(staged) * each : (len(staged) + 1) * each]
        held = call(
            functools.partial(stage_kernel, slots),
            "stage",
            pltpu.VMEM((each, depth, width), BF16),
            (weight, after),
            in_specs=[ANY_SPEC, VMEM_SPEC],
            scratch=[pltpu.SemaphoreType.DMA((each,))],
            cost=4 * MIB,
        )
        staged.append((slots, held))
        return held

    got = exchanged(queries, 1 << (bits - 1))
    stored, limit, have = call(
        functools.partial(stage_cache_kernel, tp // kv_heads),
        "stage_cache",
        [
            pltpu.VMEM(kv_cache.shape[1:], BF16),
            pltpu.VMEM((rows, span), jnp.int32),
            pltpu.VMEM(queries.shape, BF16),
        ],
        (in_hbm(lengths), in_hbm(new_kv), in_hbm(kv_cache), in_hbm(queries)),
        in_specs=[ANY_SPEC] * 4,
        scratch=[
            pltpu.SMEM(lengths.shape, jnp.int32),
            pltpu.VMEM(new_kv.shape[1:], BF16),
            pltpu.VMEM(kv_cache.shape[1:], BF16),
            pltpu.SemaphoreType.DMA((4,)),
        ],
        cost=4 * MIB,
    )
    after = limit
    for b in reversed(range(bits - 1)):
        count = 2 * have.shape[0]
        have = call(
            append_kernel, "append", struct((count, rows, heads, dim), BF16), (have, got, after)
        )
        got = exchanged(have, 1 << b)
        after = stage(have)
    packed_block = (heads * rows + STAT_ROWS, dim)
    send, kept = call(
        attention_kernel,
        "attention",
        [struct((half, *packed_block), BF16)] * 2,
        (have, got, stored, limit, after),
        scratch=[pltpu.VMEM((heads * tp, rows, span), F32)] * 2,
        cost=8 * MIB,
    )
    got = exchanged(send, 1)
    after = stage(send)
    for b in range(1, bits):
        count = kept.shape[0] // 2
        send, kept = call(
            merge_kernel, "merge", [struct((count, *packed_block), BF16)] * 2, (kept, got, after)
        )
        got = exchanged(send, 1 << b)
        after = stage(send)

    where = {
        slot: (array, i) for array, (slots, _) in enumerate(staged) for i, slot in enumerate(slots)
    }
    rest = order[windows * each :]
    soon, late = rest[: tp // 8], rest[tp // 8 :]
    flat, away, held = call(
        functools.partial(
            project_away_kernel, rows, heads, [where[slot] for slot in range(1, tp, 2)], soon
        ),
        "project_away",
        [
            struct((rows, depth), BF16),
            struct((half, rows, width), BF16),
            pltpu.VMEM((len(soon), depth, width), BF16),
        ],
        (kept, got, weight, *[held for _, held in staged]),
        in_specs=[VMEM_SPEC] * 2 + [ANY_SPEC] + [VMEM_SPEC] * len(staged),
        scratch=[pltpu.SemaphoreType.DMA((len(soon),))],
        cost=16 * MIB,
    )
    got = exchanged(away, 1)
    staged.append((soon, held))
    where.update({slot: (len(staged) - 1, i) for i, slot in enumerate(soon)})
    kept = call(
        functools.partial(
            project_own_kernel,
            [where.get(slot) for slot in range(0, tp, 2)],
            late,
            list(range(half)),
        ),
        "project_own",
        struct((half, rows, width), F32),
        (flat, weight, *[held for _, held in staged]),
        in_specs=[VMEM_SPEC, ANY_SPEC] + [VMEM_SPEC] * len(staged),
        scratch=[
            pltpu.VMEM((len(late), depth, width), BF16),
            pltpu.SemaphoreType.DMA((len(late),)),
        ],
        mib=14,
        cost=16 * MIB,
    )
    for b in range(1, bits - 1):
        slots = kept.shape[0] // 2
        send, kept = call(
            split_kernel,
            "split_sum",
            [struct((slots, rows, width), BF16), struct((slots, rows, width), F32)],
            (kept, got),
        )
        got = exchanged(send, 1 << b)
    high = 1 << (bits - 1)
    total = call(
        total_kernel, "pair_sum", struct((2, rows, width), BF16), (kept, got, residual)
    )
    far = exchanged(total, high, 1)
    near = exchanged(total, 0, 1)
    own = call(owner_kernel, "owner", struct((2, rows, width), BF16), (near, far))
    parts = [(0, own)]
    for b in reversed(range(bits - 1)):
        parts += [(offset ^ (1 << b), exchanged(part, 1 << b)) for offset, part in parts]
    return call(
        functools.partial(place_kernel, [offset for offset, _ in parts], high),
        "placed",
        struct((1, rows, full), BF16),
        [part for _, part in parts],
    )


def solution(mesh):
    return jax.shard_map(
        functools.partial(local, mesh.shape["tp"], mesh.shape["section"]),
        mesh=mesh,
        in_specs=(
            P("section", "rep", "tp", None),
            P("section", "rep", None, None, None),
            P("section", "rep", None, None, "tp", None),
            P("section", "rep"),
            P("section", "rep", "tp"),
            P("section", "tp", None),
        ),
        out_specs=P("section", "rep", None),
        check_vma=False,
    )
```

profile of v0, /device:TPU:0, one launch (start us, length us, event | category | flops | bytes accessed | tf_op | source)
XLA Modules:
  0.0 61.4 jit_solution(13172683320161164862)
XLA Ops:
  0.0 4.0 %collective-permute-start = (bf16[1,8,8,128]{3,2,1,0:T(8,128)(2,1)}, bf16[1,8,8,128]{3,2,1,0:T(8,128)(2,1)S(1)}, u32[]{:S(2)}, u32[]{:S(2)}) collective-permute-start(bf16[1,8,8,128]{3,2,1,0:T(8,128)(2,1)} %queries_ref.1), channel_id=1, source_target_pairs={{0,4},{1,5},{2,6},{3,7},{4,0},{5,1},{6,2},{7,3},{8,12},{9,13},{10,... | collective-permute-start | bytes 49160 | tf_op jit(solution)/shard_map/ppermute | solution.py:304
  4.0 2.1 %stage_cache.1 = (bf16[8,2,4,128,128]{4,3,2,1,0:T(8,128)(2,1)S(1)}, s32[8,128]{1,0:T(8,128)S(1)}, bf16[1,8,8,128]{3,2,1,0:T(8,128)(2,1)S(1)}) custom-call(s32[1,8]{1,0:T(1,128)} %lengths_ref.1, bf16[1,8,2,4,128]{4,3,2,1,0:T(4,128)(2,1)} %new_ref.1, bf16[1,8,2,4,128,128]{5,4,3,2,1,0:T(8,128)(2,1)} %kv_ref.1, bf16[1,8,8,128]{3,2,1,0:T(8,128)(2,1)} %queries_ref.1), custom_call_target="tpu_custom_call" | custom-call | flops 4194304 | bytes 4194304 | tf_op jit(solution)/shard_map/stage_cache/pallas_call | solution.py:273
  6.2 1.7 %collective-permute-start.1 = (bf16[2,8,8,128]{3,2,1,0:T(8,128)(2,1)S(1)}, bf16[2,8,8,128]{3,2,1,0:T(8,128)(2,1)S(1)}, u32[]{:S(2)}, u32[]{:S(2)}) collective-permute-start(bf16[2,8,8,128]{3,2,1,0:T(8,128)(2,1)S(1)} %append.2.after_ref.first_ref), channel_id=1, source_target_pairs={{0,2},{1,3},{2,0},{3,1},{4,6},{5,7},{6,4},{7,5},{8,10},{9,11},{10,... | collective-permute-start | bytes 98312 | tf_op jit(solution)/shard_map/ppermute | solution.py:304
  7.9 2.2 %stage.5.after_ref.refs_0_ = bf16[1,1024,2048]{2,1,0:T(8,128)(2,1)S(1)} custom-call(bf16[1,1024,16384]{2,1,0:T(8,128)(2,1)} %weight_ref.13, bf16[2,8,8,128]{3,2,1,0:T(8,128)(2,1)S(1)} %append.2.after_ref.first_ref), custom_call_target="tpu_custom_call" | custom-call | flops 4194304 | bytes 4194304 | tf_op jit(solution)/shard_map/stage/pallas_call | solution.py:273
  10.2 1.6 %collective-permute-start.2 = (bf16[4,8,8,128]{3,2,1,0:T(8,128)(2,1)S(1)}, bf16[4,8,8,128]{3,2,1,0:T(8,128)(2,1)S(1)}, u32[]{:S(2)}, u32[]{:S(2)}) collective-permute-start(bf16[4,8,8,128]{3,2,1,0:T(8,128)(2,1)S(1)} %append.3.after_ref.low_ref), channel_id=1, source_target_pairs={{0,1},{1,0},{2,3},{3,2},{4,5},{5,4},{6,7},{7,6},{8,9},{9,8},{10,11... | collective-permute-start | bytes 196616 | tf_op jit(solution)/shard_map/ppermute | solution.py:304
  11.8 2.2 %stage.6.after_ref.refs_1_ = bf16[1,1024,2048]{2,1,0:T(8,128)(2,1)S(1)} custom-call(bf16[1,1024,16384]{2,1,0:T(8,128)(2,1)} %weight_ref.13, bf16[4,8,8,128]{3,2,1,0:T(8,128)(2,1)S(1)} %append.3.after_ref.low_ref), custom_call_target="tpu_custom_call" | custom-call | flops 4194304 | bytes 4194304 | tf_op jit(solution)/shard_map/stage/pallas_call | solution.py:273
  14.5 1.1 %attention.1 = (bf16[4,80,128]{2,1,0:T(8,128)(2,1)S(1)}, bf16[4,80,128]{2,1,0:T(8,128)(2,1)S(1)}) custom-call(bf16[4,8,8,128]{3,2,1,0:T(8,128)(2,1)S(1)} %append.3.after_ref.low_ref, bf16[4,8,8,128]{3,2,1,0:T(8,128)(2,1)S(1)} %collective-permute-done.2.high_ref, bf16[8,2,4,128,128]{4,3,2,1,0:T(8,128)(2,1)S(1)} %get-tuple-element.21.stored_ref, ...), custom_call_target="tpu_custom_call" | custom-call | flops 8388608 | bytes 8388608 | tf_op jit(solution)/shard_map/attention/pallas_call | solution.py:273
  15.5 1.7 %collective-permute-start.3 = (bf16[4,80,128]{2,1,0:T(8,128)(2,1)S(1)}, bf16[4,80,128]{2,1,0:T(8,128)(2,1)S(1)}, u32[]{:S(2)}, u32[]{:S(2)}) collective-permute-start(bf16[4,80,128]{2,1,0:T(8,128)(2,1)S(1)} %get-tuple-element.23.after_ref), channel_id=1, source_target_pairs={{0,1},{1,0},{2,3},{3,2},{4,5},{5,4},{6,7},{7,6},{8,9},{9,8},{10,11... | collective-permute-start | bytes 245768 | tf_op jit(solution)/shard_map/ppermute | solution.py:304
  17.2 2.2 %stage.7.after_ref.refs_2_ = bf16[1,1024,2048]{2,1,0:T(8,128)(2,1)S(1)} custom-call(bf16[1,1024,16384]{2,1,0:T(8,128)(2,1)} %weight_ref.13, bf16[4,80,128]{2,1,0:T(8,128)(2,1)S(1)} %get-tuple-element.23.after_ref), custom_call_target="tpu_custom_call" | custom-call | flops 4194304 | bytes 4194304 | tf_op jit(solution)/shard_map/stage/pallas_call | solution.py:273
  19.4 0.6 %collective-permute-done.3.got_ref = bf16[4,80,128]{2,1,0:T(8,128)(2,1)S(1)} collective-permute-done((bf16[4,80,128]{2,1,0:T(8,128)(2,1)S(1)}, bf16[4,80,128]{2,1,0:T(8,128)(2,1)S(1)}, u32[]{:S(2)}, u32[]{:S(2)}) %collective-permute-start.3) | collective-permute-done | bytes 81952 | tf_op jit(solution)/shard_map/ppermute | solution.py:304
  20.2 1.7 %collective-permute-start.4 = (bf16[2,80,128]{2,1,0:T(8,128)(2,1)S(1)}, bf16[2,80,128]{2,1,0:T(8,128)(2,1)S(1)}, u32[]{:S(2)}, u32[]{:S(2)}) collective-permute-start(bf16[2,80,128]{2,1,0:T(8,128)(2,1)S(1)} %get-tuple-element.25.after_ref), channel_id=1, source_target_pairs={{0,2},{1,3},{2,0},{3,1},{4,6},{5,7},{6,4},{7,5},{8,10},{9,11},{10,... | collective-permute-start | bytes 122888 | tf_op jit(solution)/shard_map/ppermute | solution.py:304
  21.9 2.2 %stage.8.after_ref.refs_3_ = bf16[1,1024,2048]{2,1,0:T(8,128)(2,1)S(1)} custom-call(bf16[1,1024,16384]{2,1,0:T(8,128)(2,1)} %weight_ref.13, bf16[2,80,128]{2,1,0:T(8,128)(2,1)S(1)} %get-tuple-element.25.after_ref), custom_call_target="tpu_custom_call" | custom-call | flops 4194304 | bytes 4194304 | tf_op jit(solution)/shard_map/stage/pallas_call | solution.py:273
  24.6 2.5 %collective-permute-start.5 = (bf16[1,80,128]{2,1,0:T(8,128)(2,1)S(1)}, bf16[1,80,128]{2,1,0:T(8,128)(2,1)S(1)}, u32[]{:S(2)}, u32[]{:S(2)}) collective-permute-start(bf16[1,80,128]{2,1,0:T(8,128)(2,1)S(1)} %get-tuple-element.27.after_ref), channel_id=1, source_target_pairs={{0,4},{1,5},{2,6},{3,7},{4,0},{5,1},{6,2},{7,3},{8,12},{9,13},{10,... | collective-permute-start | bytes 61448 | tf_op jit(solution)/shard_map/ppermute | solution.py:304
  27.1 2.2 %stage.9.refs_4_ = bf16[1,1024,2048]{2,1,0:T(8,128)(2,1)S(1)} custom-call(bf16[1,1024,16384]{2,1,0:T(8,128)(2,1)} %weight_ref.13, bf16[1,80,128]{2,1,0:T(8,128)(2,1)S(1)} %get-tuple-element.27.after_ref), custom_call_target="tpu_custom_call" | custom-call | flops 4194304 | bytes 4194304 | tf_op jit(solution)/shard_map/stage/pallas_call | solution.py:273
  29.4 4.4 %project_away.1 = (bf16[8,1024]{1,0:T(8,128)(2,1)S(1)}, bf16[4,8,2048]{2,1,0:T(8,128)(2,1)S(1)}, bf16[1,1024,2048]{2,1,0:T(8,128)(2,1)S(1)}) custom-call(bf16[1,80,128]{2,1,0:T(8,128)(2,1)S(1)} %get-tuple-element.26.kept_ref, bf16[1,80,128]{2,1,0:T(8,128)(2,1)S(1)} %collective-permute-done.5.got_ref, bf16[1,1024,16384]{2,1,0:T(8,128)(2,1)} %weight_ref.13, ...), custom_call_target="tpu_custom_call" | custom-call | flops 16777216 | bytes 16777216 | tf_op jit(solution)/shard_map/project_away/pallas_call | solution.py:273
  33.8 1.7 %collective-permute-start.6 = (bf16[4,8,2048]{2,1,0:T(8,128)(2,1)S(1)}, bf16[4,8,2048]{2,1,0:T(8,128)(2,1)S(1)}, u32[]{:S(2)}, u32[]{:S(2)}) collective-permute-start(bf16[4,8,2048]{2,1,0:T(8,128)(2,1)S(1)} %get-tuple-element.30), channel_id=1, source_target_pairs={{0,1},{1,0},{2,3},{3,2},{4,5},{5,4},{6,7},{7,6},{8,9},{9,8},{10,11... | collective-permute-start | bytes 393224 | tf_op jit(solution)/shard_map/ppermute | solution.py:304
  35.5 5.3 %project_own.1.kept_ref = f32[4,8,2048]{2,1,0:T(8,128)S(1)} custom-call(bf16[8,1024]{1,0:T(8,128)(2,1)S(1)} %get-tuple-element.28.flat_ref, bf16[1,1024,16384]{2,1,0:T(8,128)(2,1)} %weight_ref.13, bf16[1,1024,2048]{2,1,0:T(8,128)(2,1)S(1)} %stage.5.after_ref.refs_0_, bf16[1,1024,2048]{2,1,0:T(8,128)(2,1)S(1)} %stage.6.after_ref.refs_1_, ...), custom_call_target="tpu_custom_call" | custom-call | flops 16777216 | bytes 16777216 | tf_op jit(solution)/shard_map/project_own/pallas_call | solution.py:273
  40.8 1.6 %collective-permute-start.7 = (bf16[2,8,2048]{2,1,0:T(8,128)(2,1)S(1)}, bf16[2,8,2048]{2,1,0:T(8,128)(2,1)S(1)}, u32[]{:S(2)}, u32[]{:S(2)}) collective-permute-start(bf16[2,8,2048]{2,1,0:T(8,128)(2,1)S(1)} %get-tuple-element.32), channel_id=1, source_target_pairs={{0,2},{1,3},{2,0},{3,1},{4,6},{5,7},{6,4},{7,5},{8,10},{9,11},{10,... | collective-permute-start | bytes 196616 | tf_op jit(solution)/shard_map/ppermute | solution.py:304
  42.4 2.8 %collective-permute-done.7.got_ref = bf16[2,8,2048]{2,1,0:T(8,128)(2,1)S(1)} collective-permute-done((bf16[2,8,2048]{2,1,0:T(8,128)(2,1)S(1)}, bf16[2,8,2048]{2,1,0:T(8,128)(2,1)S(1)}, u32[]{:S(2)}, u32[]{:S(2)}) %collective-permute-start.7) | collective-permute-done | bytes 65568 | tf_op jit(solution)/shard_map/ppermute | solution.py:304
  45.3 2.4 %collective-permute-start.8 = (bf16[2,8,2048]{2,1,0:T(8,128)(2,1)S(1)}, bf16[2,8,2048]{2,1,0:T(8,128)(2,1)S(1)}, u32[]{:S(2)}, u32[]{:S(2)}) collective-permute-start(bf16[2,8,2048]{2,1,0:T(8,128)(2,1)S(1)} %pair_sum.1), channel_id=1, source_target_pairs={{0,8},{1,9},{2,10},{3,11},{4,12},{5,13},{6,14},{7,15},{8,0},{9,1},... | collective-permute-start | bytes 196616 | tf_op jit(solution)/shard_map/ppermute | solution.py:304
  47.7 4.2 %collective-permute-done.9.far_ref = bf16[2,8,2048]{2,1,0:T(8,128)(2,1)S(1)} collective-permute-done((bf16[2,8,2048]{2,1,0:T(8,128)(2,1)S(1)}, bf16[2,8,2048]{2,1,0:T(8,128)(2,1)S(1)}, u32[]{:S(2)}, u32[]{:S(2)}) %collective-permute-start.9) | collective-permute-done | bytes 65568 | tf_op jit(solution)/shard_map/ppermute | solution.py:304
  52.7 3.8 %collective-permute-done.10.refs_1_ = bf16[2,8,2048]{2,1,0:T(8,128)(2,1)S(1)} collective-permute-done((bf16[2,8,2048]{2,1,0:T(8,128)(2,1)S(1)}, bf16[2,8,2048]{2,1,0:T(8,128)(2,1)S(1)}, u32[]{:S(2)}, u32[]{:S(2)}) %collective-permute-start.10) | collective-permute-done | bytes 65568 | tf_op jit(solution)/shard_map/ppermute | solution.py:304
  56.8 3.9 %collective-permute-done.12.refs_3_ = bf16[2,8,2048]{2,1,0:T(8,128)(2,1)S(1)} collective-permute-done((bf16[2,8,2048]{2,1,0:T(8,128)(2,1)S(1)}, bf16[2,8,2048]{2,1,0:T(8,128)(2,1)S(1)}, u32[]{:S(2)}, u32[]{:S(2)}) %collective-permute-start.12) | collective-permute-done | bytes 65568 | tf_op jit(solution)/shard_map/ppermute | solution.py:304
  60.7 0.7 %placed.1 = bf16[1,8,16384]{2,1,0:T(8,128)(2,1)} custom-call(bf16[2,8,2048]{2,1,0:T(8,128)(2,1)S(1)} %owner.1.refs_0_, bf16[2,8,2048]{2,1,0:T(8,128)(2,1)S(1)} %collective-permute-done.10.refs_1_, bf16[2,8,2048]{2,1,0:T(8,128)(2,1)S(1)} %collective-permute-done.11.refs_2_, bf16[2,8,2048]{2,1,0:T(8,128)(2,1)S(1)} %collective-permute-done.12.refs_3_), custom_call_target="tpu_custom_call" | custom-call | flops 1048576 | bytes 1048576 | tf_op jit(solution)/shard_map/placed/pallas_call | solution.py:273
  (21 shorter events, 2.5 us)
Async XLA Ops:
  0.0 6.2 %collective-permute-start = (bf16[1,8,8,128]{3,2,1,0:T(8,128)(2,1)}, bf16[1,8,8,128]{3,2,1,0:T(8,128)(2,1)S(1)}, u32[]{:S(2)}, u32[]{:S(2)}) collective-permute-start(bf16[1,8,8,128]{3,2,1,0:T(8,128)(2,1)} %queries_ref.1), channel_id=1, source_target_pairs={{0,4},{1,5},{2,6},{3,7},{4,0},{5,1},{6,2},{7,3},{8,12},{9,13},{10,... | collective-permute-start | bytes 49160 | tf_op jit(solution)/shard_map/ppermute | solution.py:304
  6.2 4.0 %collective-permute-start.1 = (bf16[2,8,8,128]{3,2,1,0:T(8,128)(2,1)S(1)}, bf16[2,8,8,128]{3,2,1,0:T(8,128)(2,1)S(1)}, u32[]{:S(2)}, u32[]{:S(2)}) collective-permute-start(bf16[2,8,8,128]{3,2,1,0:T(8,128)(2,1)S(1)} %append.2.after_ref.first_ref), channel_id=1, source_target_pairs={{0,2},{1,3},{2,0},{3,1},{4,6},{5,7},{6,4},{7,5},{8,10},{9,11},{10,... | collective-permute-start | bytes 98312 | tf_op jit(solution)/shard_map/ppermute | solution.py:304
  10.2 4.3 %collective-permute-start.2 = (bf16[4,8,8,128]{3,2,1,0:T(8,128)(2,1)S(1)}, bf16[4,8,8,128]{3,2,1,0:T(8,128)(2,1)S(1)}, u32[]{:S(2)}, u32[]{:S(2)}) collective-permute-start(bf16[4,8,8,128]{3,2,1,0:T(8,128)(2,1)S(1)} %append.3.after_ref.low_ref), channel_id=1, source_target_pairs={{0,1},{1,0},{2,3},{3,2},{4,5},{5,4},{6,7},{7,6},{8,9},{9,8},{10,11... | collective-permute-start | bytes 196616 | tf_op jit(solution)/shard_map/ppermute | solution.py:304
  15.5 4.5 %collective-permute-start.3 = (bf16[4,80,128]{2,1,0:T(8,128)(2,1)S(1)}, bf16[4,80,128]{2,1,0:T(8,128)(2,1)S(1)}, u32[]{:S(2)}, u32[]{:S(2)}) collective-permute-start(bf16[4,80,128]{2,1,0:T(8,128)(2,1)S(1)} %get-tuple-element.23.after_ref), channel_id=1, source_target_pairs={{0,1},{1,0},{2,3},{3,2},{4,5},{5,4},{6,7},{7,6},{8,9},{9,8},{10,11... | collective-permute-start | bytes 245768 | tf_op jit(solution)/shard_map/ppermute | solution.py:304
  20.2 4.3 %collective-permute-start.4 = (bf16[2,80,128]{2,1,0:T(8,128)(2,1)S(1)}, bf16[2,80,128]{2,1,0:T(8,128)(2,1)S(1)}, u32[]{:S(2)}, u32[]{:S(2)}) collective-permute-start(bf16[2,80,128]{2,1,0:T(8,128)(2,1)S(1)} %get-tuple-element.25.after_ref), channel_id=1, source_target_pairs={{0,2},{1,3},{2,0},{3,1},{4,6},{5,7},{6,4},{7,5},{8,10},{9,11},{10,... | collective-permute-start | bytes 122888 | tf_op jit(solution)/shard_map/ppermute | solution.py:304
  24.6 4.7 %collective-permute-start.5 = (bf16[1,80,128]{2,1,0:T(8,128)(2,1)S(1)}, bf16[1,80,128]{2,1,0:T(8,128)(2,1)S(1)}, u32[]{:S(2)}, u32[]{:S(2)}) collective-permute-start(bf16[1,80,128]{2,1,0:T(8,128)(2,1)S(1)} %get-tuple-element.27.after_ref), channel_id=1, source_target_pairs={{0,4},{1,5},{2,6},{3,7},{4,0},{5,1},{6,2},{7,3},{8,12},{9,13},{10,... | collective-permute-start | bytes 61448 | tf_op jit(solution)/shard_map/ppermute | solution.py:304
  33.8 7.0 %collective-permute-start.6 = (bf16[4,8,2048]{2,1,0:T(8,128)(2,1)S(1)}, bf16[4,8,2048]{2,1,0:T(8,128)(2,1)S(1)}, u32[]{:S(2)}, u32[]{:S(2)}) collective-permute-start(bf16[4,8,2048]{2,1,0:T(8,128)(2,1)S(1)} %get-tuple-element.30), channel_id=1, source_target_pairs={{0,1},{1,0},{2,3},{3,2},{4,5},{5,4},{6,7},{7,6},{8,9},{9,8},{10,11... | collective-permute-start | bytes 393224 | tf_op jit(solution)/shard_map/ppermute | solution.py:304
  35.5 9.7 %copy-start = (bf16[1,8,2048]{2,1,0:T(8,128)(2,1)S(1)}, bf16[1,8,2048]{2,1,0:T(8,128)(2,1)}, u32[]{:S(2)}) copy-start(bf16[1,8,2048]{2,1,0:T(8,128)(2,1)} %residual_ref.1) | copy-start | bytes 98308
  40.8 4.3 %collective-permute-start.7 = (bf16[2,8,2048]{2,1,0:T(8,128)(2,1)S(1)}, bf16[2,8,2048]{2,1,0:T(8,128)(2,1)S(1)}, u32[]{:S(2)}, u32[]{:S(2)}) collective-permute-start(bf16[2,8,2048]{2,1,0:T(8,128)(2,1)S(1)} %get-tuple-element.32), channel_id=1, source_target_pairs={{0,2},{1,3},{2,0},{3,1},{4,6},{5,7},{6,4},{7,5},{8,10},{9,11},{10,... | collective-permute-start | bytes 196616 | tf_op jit(solution)/shard_map/ppermute | solution.py:304
  45.2 6.8 %collective-permute-start.9 = (bf16[2,8,2048]{2,1,0:T(8,128)(2,1)S(1)}, bf16[2,8,2048]{2,1,0:T(8,128)(2,1)S(1)}, u32[]{:S(2)}, u32[]{:S(2)}) collective-permute-start(bf16[2,8,2048]{2,1,0:T(8,128)(2,1)S(1)} %pair_sum.1), channel_id=1, source_target_pairs={{0,12},{1,13},{2,14},{3,15},{4,8},{5,9},{6,10},{7,11},{8,4},{9,5},... | collective-permute-start | bytes 196616 | tf_op jit(solution)/shard_map/ppermute | solution.py:304
  45.3 6.7 %collective-permute-start.8 = (bf16[2,8,2048]{2,1,0:T(8,128)(2,1)S(1)}, bf16[2,8,2048]{2,1,0:T(8,128)(2,1)S(1)}, u32[]{:S(2)}, u32[]{:S(2)}) collective-permute-start(bf16[2,8,2048]{2,1,0:T(8,128)(2,1)S(1)} %pair_sum.1), channel_id=1, source_target_pairs={{0,8},{1,9},{2,10},{3,11},{4,12},{5,13},{6,14},{7,15},{8,0},{9,1},... | collective-permute-start | bytes 196616 | tf_op jit(solution)/shard_map/ppermute | solution.py:304
  52.1 4.3 %collective-permute-start.10 = (bf16[2,8,2048]{2,1,0:T(8,128)(2,1)S(1)}, bf16[2,8,2048]{2,1,0:T(8,128)(2,1)S(1)}, u32[]{:S(2)}, u32[]{:S(2)}) collective-permute-start(bf16[2,8,2048]{2,1,0:T(8,128)(2,1)S(1)} %owner.1.refs_0_), channel_id=1, source_target_pairs={{0,2},{1,3},{2,0},{3,1},{4,6},{5,7},{6,4},{7,5},{8,10},{9,11},{10,... | collective-permute-start | bytes 196616 | tf_op jit(solution)/shard_map/ppermute | solution.py:304
  52.2 4.6 %collective-permute-start.11 = (bf16[2,8,2048]{2,1,0:T(8,128)(2,1)S(1)}, bf16[2,8,2048]{2,1,0:T(8,128)(2,1)S(1)}, u32[]{:S(2)}, u32[]{:S(2)}) collective-permute-start(bf16[2,8,2048]{2,1,0:T(8,128)(2,1)S(1)} %owner.1.refs_0_), channel_id=1, source_target_pairs={{0,1},{1,0},{2,3},{3,2},{4,5},{5,4},{6,7},{7,6},{8,9},{9,8},{10,11... | collective-permute-start | bytes 196616 | tf_op jit(solution)/shard_map/ppermute | solution.py:304
  56.4 4.3 %collective-permute-start.12 = (bf16[2,8,2048]{2,1,0:T(8,128)(2,1)S(1)}, bf16[2,8,2048]{2,1,0:T(8,128)(2,1)S(1)}, u32[]{:S(2)}, u32[]{:S(2)}) collective-permute-start(bf16[2,8,2048]{2,1,0:T(8,128)(2,1)S(1)} %collective-permute-done.10.refs_1_), channel_id=1, source_target_pairs={{0,1},{1,0},{2,3},{3,2},{4,5},{5,4},{6,7},{7,6},{8,9},{9,8},{10,11... | collective-permute-start | bytes 196616 | tf_op jit(solution)/shard_map/ppermute | solution.py:304
where the time goes:
time: 61.8 us; the launch traced here: 61.4 us
  Pallas kernels  25.1 us (41%)
  starting transfers between devices  19.8 us (32%)
  waiting for transfers between devices  16.4 us (27%)
    pallas_call x17, Pallas kernels, call(): pl.pallas_call(kernel, out_shape=outs, in_specs=in_specs or [VMEM_SPEC] *...  25.1 us
    ppermute x13, starting transfers between devices, exchanged(): return lax.ppermute(array, ('section', 'tp'), pairs)  19.8 us
    ppermute x13, waiting for transfers between devices, exchanged(): return lax.ppermute(array, ('section', 'tp'), pairs)  16.4 us
  transfers between devices with their start and end apart: 13, of which 9 were waited for; matrix products, arithmetic and copies ran while one was open for 0% of the time, Pallas kernels for 30%

commit v1 on v0

v1 whole, which is shorter than its diff:
```python
import functools
import math

import jax
import jax.numpy as jnp
from jax import lax
from jax.experimental import pallas as pl
from jax.experimental.pallas import tpu as pltpu
from jax.sharding import PartitionSpec as P

QB = 128
LANES = 128
STAT_ROWS = 16
MIB = 1 << 20
F32 = jnp.float32
BF16 = jnp.bfloat16
VMEM_SPEC = pl.BlockSpec(memory_space=pltpu.VMEM)
ANY_SPEC = pl.BlockSpec(memory_space=pl.ANY)


def pieces(x):
    high = x.astype(BF16).astype(F32)
    rest = x - high
    middle = rest.astype(BF16).astype(F32)
    return high, middle, rest - middle


def weight_copies(slots, weight_ref, held_ref, sems, cuts=1):
    rank = lax.axis_index("tp")
    width = held_ref.shape[2]
    piece = width // cuts
    copies = []
    for i, slot in enumerate(slots):
        for c in range(cuts):
            start = pl.multiple_of((rank ^ slot) * width + c * piece, piece)
            copies.append(
                pltpu.make_async_copy(
                    weight_ref.at[0, :, pl.ds(start, piece)],
                    held_ref.at[i, :, c * piece : (c + 1) * piece],
                    sems.at[i * cuts + c],
                )
            )
    return copies


def stage_cache_kernel(
    per, slots, lengths_ref, new_ref, kv_ref, queries_ref, weight_ref,
    stored_ref, limit_ref, near_ref, held_ref, lengths, new, kv, sems, held_sems,
):
    rank = lax.axis_index("tp")
    rows, _, kv_heads, span, dim = kv.shape
    copies = [
        pltpu.make_async_copy(lengths_ref, lengths, sems.at[0]),
        pltpu.make_async_copy(new_ref.at[0], new, sems.at[1]),
        pltpu.make_async_copy(kv_ref.at[0], kv, sems.at[2]),
        pltpu.make_async_copy(queries_ref, near_ref, sems.at[3]),
    ]
    held = weight_copies(slots, weight_ref, held_ref, held_sems)
    for copy in copies + held:
        copy.start()
    for copy in copies:
        copy.wait()
    first = rank * span
    sub = lax.broadcasted_iota(jnp.int32, (span, dim), 0)
    kv_sub = lax.broadcasted_iota(jnp.int32, (kv_heads, dim), 0)
    row_of = lax.broadcasted_iota(jnp.int32, (rows, span), 0)
    limit = jnp.zeros((rows, span), jnp.int32)
    for r in range(rows):
        limit = jnp.where(row_of == r, lengths[0, r] - first, limit)
        written = sub == lengths[0, r] - first
        for which in range(2):
            new_heads = new[r, which].astype(F32)
            for m in range(kv_heads):
                head = (rank // per) ^ m
                fresh = jnp.sum(
                    jnp.where(kv_sub == head, new_heads, 0.0), axis=0, keepdims=True
                )
                block = kv[r, which, head].astype(F32)
                stored_ref[r, which, m] = jnp.where(written, fresh, block).astype(BF16)
    limit_ref[...] = limit
    for copy in held:
        copy.wait()


def stage_kernel(slots, weight_ref, after_ref, held_ref, sems):
    del after_ref
    copies = weight_copies(slots, weight_ref, held_ref, sems)
    for copy in copies:
        copy.start()
    for copy in copies:
        copy.wait()


def append_kernel(first_ref, second_ref, after_ref, out_ref):
    del after_ref
    count = first_ref.shape[0]
    out_ref[:count] = first_ref[...]
    out_ref[count:] = second_ref[...]


def packed(mixed, top, total):
    stat_sub = lax.broadcasted_iota(jnp.int32, (STAT_ROWS, LANES), 0)
    tile = jnp.zeros((STAT_ROWS, LANES), F32)
    for i, piece in enumerate(pieces(top) + pieces(total)):
        tile = jnp.where(stat_sub == i, piece, tile)
    return jnp.concatenate([mixed, tile], axis=0).astype(BF16)


def to_lanes(column):
    n = column.shape[0]
    sub = lax.broadcasted_iota(jnp.int32, (n, LANES), 0)
    lane = lax.broadcasted_iota(jnp.int32, (n, LANES), 1)
    return jnp.sum(jnp.where(lane == sub, column, 0.0), axis=0, keepdims=True)


def to_column(row, n):
    sub = lax.broadcasted_iota(jnp.int32, (n, LANES), 0)
    lane = lax.broadcasted_iota(jnp.int32, (n, LANES), 1)
    return jnp.sum(jnp.where(lane == sub, row, 0.0), axis=1, keepdims=True)


def merged(blocks):
    n = blocks[0].shape[0] - STAT_ROWS
    tops, sums = [], []
    for block in blocks:
        tile = block[n:].astype(F32)
        tops.append(tile[0:1] + tile[1:2] + tile[2:3])
        sums.append(tile[3:4] + tile[4:5] + tile[5:6])
    top = functools.reduce(jnp.maximum, tops)
    mixed, total = 0.0, 0.0
    for block, own_top, own_sum in zip(blocks, tops, sums):
        factor = jnp.exp(own_top - top)
        total = total + own_sum * factor
        mixed = mixed + block[:n].astype(F32) * to_column(factor, n)
    return mixed, top, total


def attention_kernel(stored_ref, limit_ref, after_ref, *refs):
    del after_ref
    sources, outs, (scores_ref, mixed_ref) = refs[:4], refs[4:8], refs[8:]
    quarter, rows, heads, dim = sources[0].shape
    tp = 4 * quarter
    kv_heads, span = stored_ref.shape[2:4]
    group = heads * tp // kv_heads
    per = group // heads
    scale = 1.0 / math.sqrt(dim)

    def query(k, r):
        return sources[k // quarter][k % quarter, r].astype(F32)

    for m in range(kv_heads):
        for r in range(rows):
            q = jnp.concatenate([query(m * per + i, r) for i in range(per)], axis=0).astype(BF16)
            s = lax.dot_general(
                q, stored_ref[r, 0, m], (((1,), (1,)), ((), ())), preferred_element_type=F32
            )
            scores_ref[m * group : (m + 1) * group, r, :] = s * scale

    pos = lax.broadcasted_iota(jnp.int32, (rows, span), 1)
    visible = (pos <= limit_ref[...])[None]
    scores = jnp.where(visible, scores_ref[...], -1e30)
    top = jnp.max(scores, axis=-1, keepdims=True)
    weights = jnp.where(visible, jnp.exp(scores - top), 0.0)
    total = jnp.sum(weights, axis=-1, keepdims=True)
    scores_ref[...] = weights

    for m in range(kv_heads):
        for r in range(rows):
            w = scores_ref[m * group : (m + 1) * group, r, :].astype(BF16)
            mixed_ref[m * group : (m + 1) * group, r, :] = jnp.dot(
                w, stored_ref[r, 1, m], preferred_element_type=F32
            )

    n = heads * rows
    for k in range(tp):
        own = slice(k * heads, (k + 1) * heads)
        outs[k // quarter][k % quarter] = packed(
            mixed_ref[own].reshape(n, dim),
            to_lanes(top[own].reshape(n, 1)),
            to_lanes(total[own].reshape(n, 1)),
        )


def merge_kernel(after_ref, *refs):
    del after_ref
    sources, (send_ref, keep_ref) = refs[:-2], refs[-2:]
    count = keep_ref.shape[0]
    for i in range(2 * count):
        block = packed(*merged([source[i] for source in sources]))
        if i < count:
            keep_ref[i] = block
        else:
            send_ref[i - count] = block


def requantized(x):
    top = jnp.max(jnp.abs(x), axis=-1, keepdims=True)
    scale = ((top + 1e-06) / 127.0).astype(BF16).astype(F32)
    return jnp.clip(jnp.floor(x / scale + 0.5), -127.0, 127.0) * scale


def project_columns(flat, weight, out_ref, i, start):
    columns = weight.shape[1]
    tile = min(512, columns)
    for c in range(0, columns, tile):
        part = jnp.dot(flat, weight[:, c : c + tile], preferred_element_type=F32)
        for b in range(0, tile, QB):
            at = start + c + b
            block = requantized(part[:, b : b + QB])
            out_ref[i, :, at : at + QB] = block.astype(out_ref.dtype)


def project_away_kernel(rows, heads, places, kept_ref, got_ref, *refs):
    held, (flat_ref, out_ref) = refs[:-2], refs[-2:]
    mixed, _, total = merged([kept_ref[0], got_ref[0]])
    attended = mixed / to_column(total, mixed.shape[0])
    flat = jnp.concatenate(
        [attended[h * rows : (h + 1) * rows] for h in range(heads)], axis=1
    ).astype(BF16)
    flat_ref[...] = flat
    for i, (array, index) in enumerate(places):
        project_columns(flat, held[array].at[index], out_ref, i, 0)


def project_own_kernel(places, slots, cuts, flat_ref, weight_ref, *refs):
    held, (out_ref, late_ref, sems) = refs[:-3], refs[-3:]
    copies = weight_copies(slots, weight_ref, late_ref, sems, cuts)
    for copy in copies:
        copy.start()
    flat = flat_ref[...]
    for i, place in enumerate(places):
        if place is not None:
            project_columns(flat, held[place[0]].at[place[1]], out_ref, i, 0)
    piece = late_ref.shape[2] // cuts
    for late, slot in enumerate(slots):
        for c in range(cuts):
            copies[late * cuts + c].wait()
            columns = late_ref.at[late, :, c * piece : (c + 1) * piece]
            project_columns(flat, columns, out_ref, slot >> 1, c * piece)


def split_kernel(kept_ref, got_ref, send_ref, keep_ref):
    for i in range(send_ref.shape[0]):
        send_ref[i] = (kept_ref[2 * i + 1] + got_ref[2 * i + 1].astype(F32)).astype(BF16)
        keep_ref[i] = kept_ref[2 * i] + got_ref[2 * i].astype(F32)


def pair_kernel(kept_ref, got_ref, residual_ref, even_ref, odd_ref):
    for i in range(4):
        x = kept_ref[i] + got_ref[i].astype(F32)
        if i == 0:
            x = x + residual_ref[0].astype(F32)
        if i & 1:
            odd_ref[i >> 1] = x.astype(BF16)
        else:
            even_ref[i >> 1] = x.astype(BF16)


def owner_kernel(near_ref, one_ref, two_ref, three_ref, out_ref):
    for i in range(2):
        for b in range(0, out_ref.shape[2], QB):
            at = slice(b, b + QB)
            x = near_ref[i, :, at].astype(F32) + one_ref[i, :, at].astype(F32)
            y = two_ref[1 - i, :, at].astype(F32) + three_ref[1 - i, :, at].astype(F32)
            out_ref[i, :, at] = requantized(x + y).astype(BF16)


def place_kernel(offsets, high, *refs):
    blocks, out_ref = refs[:-1], refs[-1]
    width = blocks[0].shape[2]
    rank = lax.axis_index("tp")
    for offset, block in zip(offsets, blocks):
        for i in range(2):
            start = pl.multiple_of((rank ^ offset ^ (i * high)) * width, width)
            out_ref[0, :, pl.ds(start, width)] = block[i]


def call(kernel, name, outs, args, in_specs=None, scratch=(), mib=4, cost=MIB):
    return pl.pallas_call(
        kernel,
        out_shape=outs,
        in_specs=in_specs or [VMEM_SPEC] * len(args),
        out_specs=jax.tree.map(lambda _: VMEM_SPEC, outs),
        scratch_shapes=scratch,
        compiler_params=pltpu.CompilerParams(vmem_limit_bytes=mib * MIB),
        cost_estimate=pl.CostEstimate(flops=cost, bytes_accessed=cost, transcendentals=0),
        name=name,
    )(*args)


def in_hbm(array):
    return pltpu.with_memory_space_constraint(array, pltpu.HBM)


def local(tp, sections, queries, new_kv, kv_cache, lengths, residual, out_weight):
    rows, heads, dim = queries.shape[1:]
    kv_heads, span = kv_cache.shape[3:5]
    depth, full = out_weight.shape[1:]
    width = full // tp
    half = tp // 2
    bits = tp.bit_length() - 1
    struct = jax.ShapeDtypeStruct

    def exchanged(array, k, shift=0):
        pairs = [
            (s * tp + t, ((s + shift) % sections) * tp + (t ^ k))
            for s in range(sections)
            for t in range(tp)
        ]
        return lax.ppermute(array, ("section", "tp"), pairs)

    weight = in_hbm(out_weight)
    quarter = tp // 4
    groups = [g * quarter for g in range(1, 4)]
    order = list(range(1, tp, 2)) + list(range(0, tp, 2))
    each = tp // 8
    staged = []

    def next_slots(count):
        used = sum(len(slots) for slots, _ in staged)
        return order[used : used + count * each]

    def stage(after, count):
        slots = next_slots(count)
        held = call(
            functools.partial(stage_kernel, slots),
            "stage",
            pltpu.VMEM((len(slots), depth, width), BF16),
            (weight, after),
            in_specs=[ANY_SPEC, VMEM_SPEC],
            scratch=[pltpu.SemaphoreType.DMA((len(slots),))],
            cost=4 * MIB * count,
        )
        staged.append((slots, held))
        return held

    got = exchanged(queries, 1)
    slots = next_slots(1)
    stored, limit, have, held = call(
        functools.partial(stage_cache_kernel, tp // kv_heads, slots),
        "stage_cache",
        [
            pltpu.VMEM(kv_cache.shape[1:], BF16),
            pltpu.VMEM((rows, span), jnp.int32),
            pltpu.VMEM(queries.shape, BF16),
            pltpu.VMEM((len(slots), depth, width), BF16),
        ],
        (in_hbm(lengths), in_hbm(new_kv), in_hbm(kv_cache), in_hbm(queries), weight),
        in_specs=[ANY_SPEC] * 5,
        scratch=[
            pltpu.SMEM(lengths.shape, jnp.int32),
            pltpu.VMEM(new_kv.shape[1:], BF16),
            pltpu.VMEM(kv_cache.shape[1:], BF16),
            pltpu.SemaphoreType.DMA((4,)),
            pltpu.SemaphoreType.DMA((len(slots),)),
        ],
        cost=8 * MIB,
    )
    staged.append((slots, held))
    after = limit
    for b in range(bits - 2):
        count = 2 << b
        have = call(
            append_kernel, "append", struct((count, rows, heads, dim), BF16), (have, got, after)
        )
        after = have
        if b < bits - 3:
            got = exchanged(have, 2 << b)
    all_queries = [have, *(exchanged(have, k) for k in reversed(groups))]
    all_queries[1:] = all_queries[:0:-1]
    after = stage(have, 2)
    packed_block = (heads * rows + STAT_ROWS, dim)
    partial = call(
        attention_kernel,
        "attention",
        [struct((quarter, *packed_block), BF16)] * 4,
        (stored, limit, after, *all_queries),
        scratch=[pltpu.VMEM((heads * tp, rows, span), F32)] * 2,
        cost=8 * MIB,
    )
    pending = [partial[0], *(exchanged(partial[g], g * quarter) for g in (3, 2, 1))]
    after = stage(partial[3], 2)
    for b in reversed(range(bits - 2)):
        send, kept = call(
            merge_kernel, "merge", [struct((1 << b, *packed_block), BF16)] * 2, (after, *pending)
        )
        pending = [kept, exchanged(send, 1 << b)]
        after = send
    stage(send, 1)

    where = {
        slot: (array, i) for array, (slots, _) in enumerate(staged) for i, slot in enumerate(slots)
    }
    late = next_slots(tp)
    held = [array for _, array in staged]
    cuts = max(1, width // 512)
    flat, away = call(
        functools.partial(
            project_away_kernel, rows, heads, [where[slot] for slot in range(1, tp, 2)]
        ),
        "project_away",
        [struct((rows, depth), BF16), struct((half, rows, width), BF16)],
        (*pending, *held),
        cost=16 * MIB,
    )
    got = exchanged(away, 1)
    kept = call(
        functools.partial(
            project_own_kernel, [where.get(slot) for slot in range(0, tp, 2)], late, cuts
        ),
        "project_own",
        struct((half, rows, width), F32),
        (flat, weight, *held),
        in_specs=[VMEM_SPEC, ANY_SPEC] + [VMEM_SPEC] * len(held),
        scratch=[
            pltpu.VMEM((len(late), depth, width), BF16),
            pltpu.SemaphoreType.DMA((len(late) * cuts,)),
        ],
        mib=14,
        cost=16 * MIB,
    )
    for b in range(1, bits - 2):
        slots = kept.shape[0] // 2
        send, kept = call(
            split_kernel,
            "split_sum",
            [struct((slots, rows, width), BF16), struct((slots, rows, width), F32)],
            (kept, got),
        )
        got = exchanged(send, 1 << b)
    even, odd = call(
        pair_kernel, "pair_sum", [struct((2, rows, width), BF16)] * 2, (kept, got, residual)
    )
    three = exchanged(odd, groups[2], 1)
    two = exchanged(even, groups[1], 1)
    one = exchanged(odd, groups[0], 1)
    near = exchanged(even, 0, 1)
    own = call(
        owner_kernel, "owner", struct((2, rows, width), BF16), (near, one, two, three)
    )
    high = 1 << (bits - 1)
    parts = [(0, own)] + [(k, exchanged(own, k)) for k in reversed(range(1, high))]
    return call(
        functools.partial(place_kernel, [offset for offset, _ in parts], high),
        "placed",
        struct((1, rows, full), BF16),
        [part for _, part in parts],
    )


def solution(mesh):
    return jax.shard_map(
        functools.partial(local, mesh.shape["tp"], mesh.shape["section"]),
        mesh=mesh,
        in_specs=(
            P("section", "rep", "tp", None),
            P("section", "rep", None, None, None),
            P("section", "rep", None, None, "tp", None),
            P("section", "rep"),
            P("section", "rep", "tp"),
            P("section", "tp", None),
        ),
        out_specs=P("section", "rep", None),
        check_vma=False,
    )
```

time: 61.8 us -> 52.7 us (0.85)
  waiting for transfers between devices: 16.4 us -> 9.97 us
  Pallas kernels: 25.1 us -> 21.6 us
  starting transfers between devices: 19.8 us -> 20.9 us
    ppermute x13 -> x16, waiting for transfers between devices: 16.4 us -> 9.97 us  [exchanged(): return lax.ppermute(array, ('section', 'tp'), pairs)]
    pallas_call x17 -> x12, Pallas kernels: 25.1 us -> 21.6 us  [call(): pl.pallas_call(kernel, out_shape=outs, in_specs=in_specs or [VMEM_SPEC] *...]
    ppermute x13 -> x16, starting transfers between devices: 19.8 us -> 20.9 us  [exchanged(): return lax.ppermute(array, ('section', 'tp'), pairs)]
  transfers between devices with their start and end apart: 13 -> 16, of which waited for: 9 -> 9; matrix products, arithmetic and copies ran while one was open for 0% -> 0% of each run, Pallas kernels for 30% -> 32%
where the time goes in v1:
time: 52.7 us; the launch traced here: 52.6 us
  Pallas kernels  21.6 us (41%)
  starting transfers between devices  20.9 us (40%)
  waiting for transfers between devices  9.97 us (19%)
    pallas_call x12, Pallas kernels, call(): pl.pallas_call(kernel, out_shape=outs, in_specs=in_specs or [VMEM_SPEC] *...  21.6 us
    ppermute x16, starting transfers between devices, exchanged(): return lax.ppermute(array, ('section', 'tp'), pairs)  20.9 us
    ppermute x16, waiting for transfers between devices, exchanged(): return lax.ppermute(array, ('section', 'tp'), pairs)  9.97 us
  transfers between devices with their start and end apart: 16, of which 9 were waited for; matrix products, arithmetic and copies ran while one was open for 0% of the time, Pallas kernels for 32%

profile of v1, /device:TPU:0, one launch (start us, length us, event | category | flops | bytes accessed | tf_op | source)
XLA Modules:
  0.0 52.6 jit_solution(2409920324980107664)
XLA Ops:
  0.0 3.0 %collective-permute-start = (bf16[1,8,8,128]{3,2,1,0:T(8,128)(2,1)}, bf16[1,8,8,128]{3,2,1,0:T(8,128)(2,1)S(1)}, u32[]{:S(2)}, u32[]{:S(2)}) collective-permute-start(bf16[1,8,8,128]{3,2,1,0:T(8,128)(2,1)} %queries_ref.1), channel_id=1, source_target_pairs={{0,1},{1,0},{2,3},{3,2},{4,5},{5,4},{6,7},{7,6},{8,9},{9,8},{10,11... | collective-permute-start | bytes 49160 | tf_op jit(solution)/shard_map/ppermute | solution.py:310
  3.0 2.9 %stage_cache.1 = (bf16[8,2,4,128,128]{4,3,2,1,0:T(8,128)(2,1)S(1)}, s32[8,128]{1,0:T(8,128)S(1)}, bf16[1,8,8,128]{3,2,1,0:T(8,128)(2,1)S(1)}, bf16[1,1024,2048]{2,1,0:T(8,128)(2,1)S(1)}) custom-call(s32[1,8]{1,0:T(1,128)} %lengths_ref.1, bf16[1,8,2,4,128]{4,3,2,1,0:T(4,128)(2,1)} %new_ref.1, bf16[1,8,2,4,128,128]{5,4,3,2,1,0:T(8,128)(2,1)} %kv_ref.1, ...), custom_call_target="tpu_custom_call" | custom-call | flops 8388608 | bytes 8388608 | tf_op jit(solution)/shard_map/stage_cache/pallas_call | solution.py:279
  5.9 3.7 %collective-permute-start.3 = (bf16[2,8,8,128]{3,2,1,0:T(8,128)(2,1)S(1)}, bf16[2,8,8,128]{3,2,1,0:T(8,128)(2,1)S(1)}, u32[]{:S(2)}, u32[]{:S(2)}) collective-permute-start(bf16[2,8,8,128]{3,2,1,0:T(8,128)(2,1)S(1)} %append.1.after_ref.refs_0_), channel_id=1, source_target_pairs={{0,6},{1,7},{2,4},{3,5},{4,2},{5,3},{6,0},{7,1},{8,14},{9,15},{10,... | collective-permute-start | bytes 98312 | tf_op jit(solution)/shard_map/ppermute | solution.py:310
  9.6 0.8 %collective-permute-start.1 = (bf16[2,8,8,128]{3,2,1,0:T(8,128)(2,1)S(1)}, bf16[2,8,8,128]{3,2,1,0:T(8,128)(2,1)S(1)}, u32[]{:S(2)}, u32[]{:S(2)}) collective-permute-start(bf16[2,8,8,128]{3,2,1,0:T(8,128)(2,1)S(1)} %append.1.after_ref.refs_0_), channel_id=1, source_target_pairs={{0,2},{1,3},{2,0},{3,1},{4,6},{5,7},{6,4},{7,5},{8,10},{9,11},{10,... | collective-permute-start | bytes 98312 | tf_op jit(solution)/shard_map/ppermute | solution.py:310
  10.3 3.5 %stage.3.after_ref.refs_1_ = bf16[2,1024,2048]{2,1,0:T(8,128)(2,1)S(1)} custom-call(bf16[1,1024,16384]{2,1,0:T(8,128)(2,1)} %weight_ref.9, bf16[2,8,8,128]{3,2,1,0:T(8,128)(2,1)S(1)} %append.1.after_ref.refs_0_), custom_call_target="tpu_custom_call" | custom-call | flops 8388608 | bytes 8388608 | tf_op jit(solution)/shard_map/stage/pallas_call | solution.py:279
  14.4 1.1 %attention.1 = (bf16[2,80,128]{2,1,0:T(8,128)(2,1)S(1)}, bf16[2,80,128]{2,1,0:T(8,128)(2,1)S(1)}, bf16[2,80,128]{2,1,0:T(8,128)(2,1)S(1)}, bf16[2,80,128]{2,1,0:T(8,128)(2,1)S(1)}) custom-call(bf16[8,2,4,128,128]{4,3,2,1,0:T(8,128)(2,1)S(1)} %get-tuple-element.19.stored_ref, s32[8,128]{1,0:T(8,128)S(1)} %get-tuple-element.20.after_ref.limit_ref, ...), custom_call_target="tpu_custom_call" | custom-call | flops 8388608 | bytes 8388608 | tf_op jit(solution)/shard_map/attention/pallas_call | solution.py:279
  15.5 2.1 %collective-permute-start.5 = (bf16[2,80,128]{2,1,0:T(8,128)(2,1)S(1)}, bf16[2,80,128]{2,1,0:T(8,128)(2,1)S(1)}, u32[]{:S(2)}, u32[]{:S(2)}) collective-permute-start(bf16[2,80,128]{2,1,0:T(8,128)(2,1)S(1)} %get-tuple-element.24), channel_id=1, source_target_pairs={{0,4},{1,5},{2,6},{3,7},{4,0},{5,1},{6,2},{7,3},{8,12},{9,13},{10,... | collective-permute-start | bytes 122888 | tf_op jit(solution)/shard_map/ppermute | solution.py:310
  17.6 1.6 %collective-permute-start.6 = (bf16[2,80,128]{2,1,0:T(8,128)(2,1)S(1)}, bf16[2,80,128]{2,1,0:T(8,128)(2,1)S(1)}, u32[]{:S(2)}, u32[]{:S(2)}) collective-permute-start(bf16[2,80,128]{2,1,0:T(8,128)(2,1)S(1)} %get-tuple-element.25), channel_id=1, source_target_pairs={{0,2},{1,3},{2,0},{3,1},{4,6},{5,7},{6,4},{7,5},{8,10},{9,11},{10,... | collective-permute-start | bytes 122888 | tf_op jit(solution)/shard_map/ppermute | solution.py:310
  20.0 3.5 %stage.4.after_ref.refs_2_ = bf16[2,1024,2048]{2,1,0:T(8,128)(2,1)S(1)} custom-call(bf16[1,1024,16384]{2,1,0:T(8,128)(2,1)} %weight_ref.9, bf16[2,80,128]{2,1,0:T(8,128)(2,1)S(1)} %get-tuple-element.22.after_ref), custom_call_target="tpu_custom_call" | custom-call | flops 8388608 | bytes 8388608 | tf_op jit(solution)/shard_map/stage/pallas_call | solution.py:279
  23.5 1.6 %collective-permute-done.4.refs_1_ = bf16[2,80,128]{2,1,0:T(8,128)(2,1)S(1)} collective-permute-done((bf16[2,80,128]{2,1,0:T(8,128)(2,1)S(1)}, bf16[2,80,128]{2,1,0:T(8,128)(2,1)S(1)}, u32[]{:S(2)}, u32[]{:S(2)}) %collective-permute-start.4) | collective-permute-done | bytes 40992 | tf_op jit(solution)/shard_map/ppermute | solution.py:310
  25.2 1.0 %collective-permute-start.7 = (bf16[1,80,128]{2,1,0:T(8,128)(2,1)S(1)}, bf16[1,80,128]{2,1,0:T(8,128)(2,1)S(1)}, u32[]{:S(2)}, u32[]{:S(2)}) collective-permute-start(bf16[1,80,128]{2,1,0:T(8,128)(2,1)S(1)} %get-tuple-element.27.after_ref), channel_id=1, source_target_pairs={{0,1},{1,0},{2,3},{3,2},{4,5},{5,4},{6,7},{7,6},{8,9},{9,8},{10,11... | collective-permute-start | bytes 61448 | tf_op jit(solution)/shard_map/ppermute | solution.py:310
  26.2 2.2 %stage.5.refs_3_ = bf16[1,1024,2048]{2,1,0:T(8,128)(2,1)S(1)} custom-call(bf16[1,1024,16384]{2,1,0:T(8,128)(2,1)} %weight_ref.9, bf16[1,80,128]{2,1,0:T(8,128)(2,1)S(1)} %get-tuple-element.27.after_ref), custom_call_target="tpu_custom_call" | custom-call | flops 4194304 | bytes 4194304 | tf_op jit(solution)/shard_map/stage/pallas_call | solution.py:279
  29.0 2.5 %project_away.1 = (bf16[8,1024]{1,0:T(8,128)(2,1)S(1)}, bf16[4,8,2048]{2,1,0:T(8,128)(2,1)S(1)}) custom-call(bf16[1,80,128]{2,1,0:T(8,128)(2,1)S(1)} %get-tuple-element.26.kept_ref, bf16[1,80,128]{2,1,0:T(8,128)(2,1)S(1)} %collective-permute-done.7.got_ref, bf16[1,1024,2048]{2,1,0:T(8,128)(2,1)S(1)} %get-tuple-element.28.refs_0_, ...), custom_call_target="tpu_custom_call" | custom-call | flops 16777216 | bytes 16777216 | tf_op jit(solution)/shard_map/project_away/pallas_call | solution.py:279
  31.5 1.0 %collective-permute-start.8 = (bf16[4,8,2048]{2,1,0:T(8,128)(2,1)S(1)}, bf16[4,8,2048]{2,1,0:T(8,128)(2,1)S(1)}, u32[]{:S(2)}, u32[]{:S(2)}) collective-permute-start(bf16[4,8,2048]{2,1,0:T(8,128)(2,1)S(1)} %get-tuple-element.30), channel_id=1, source_target_pairs={{0,1},{1,0},{2,3},{3,2},{4,5},{5,4},{6,7},{7,6},{8,9},{9,8},{10,11... | collective-permute-start | bytes 393224 | tf_op jit(solution)/shard_map/ppermute | solution.py:310
  32.5 4.9 %project_own.1.kept_ref = f32[4,8,2048]{2,1,0:T(8,128)S(1)} custom-call(bf16[8,1024]{1,0:T(8,128)(2,1)S(1)} %get-tuple-element.29.flat_ref, bf16[1,1024,16384]{2,1,0:T(8,128)(2,1)} %weight_ref.9, bf16[1,1024,2048]{2,1,0:T(8,128)(2,1)S(1)} %get-tuple-element.28.refs_0_, bf16[2,1024,2048]{2,1,0:T(8,128)(2,1)S(1)} %stage.3.after_ref.refs_1_, ...), custom_call_target="tpu_custom_call" | custom-call | flops 16777216 | bytes 16777216 | tf_op jit(solution)/shard_map/project_own/pallas_call | solution.py:279
  37.6 1.7 %collective-permute-start.12 = (bf16[2,8,2048]{2,1,0:T(8,128)(2,1)S(1)}, bf16[2,8,2048]{2,1,0:T(8,128)(2,1)S(1)}, u32[]{:S(2)}, u32[]{:S(2)}) collective-permute-start(bf16[2,8,2048]{2,1,0:T(8,128)(2,1)S(1)} %get-tuple-element.32), channel_id=1, source_target_pairs={{0,14},{1,15},{2,12},{3,13},{4,10},{5,11},{6,8},{7,9},{8,6},{9,7},... | collective-permute-start | bytes 196616 | tf_op jit(solution)/shard_map/ppermute | solution.py:310
  39.3 1.6 %collective-permute-start.10 = (bf16[2,8,2048]{2,1,0:T(8,128)(2,1)S(1)}, bf16[2,8,2048]{2,1,0:T(8,128)(2,1)S(1)}, u32[]{:S(2)}, u32[]{:S(2)}) collective-permute-start(bf16[2,8,2048]{2,1,0:T(8,128)(2,1)S(1)} %get-tuple-element.32), channel_id=1, source_target_pairs={{0,10},{1,11},{2,8},{3,9},{4,14},{5,15},{6,12},{7,13},{8,2},{9,3},... | collective-permute-start | bytes 196616 | tf_op jit(solution)/shard_map/ppermute | solution.py:310
  40.9 1.3 %collective-permute-done.11.two_ref = bf16[2,8,2048]{2,1,0:T(8,128)(2,1)S(1)} collective-permute-done((bf16[2,8,2048]{2,1,0:T(8,128)(2,1)S(1)}, bf16[2,8,2048]{2,1,0:T(8,128)(2,1)S(1)}, u32[]{:S(2)}, u32[]{:S(2)}) %collective-permute-start.11) | collective-permute-done | bytes 65568 | tf_op jit(solution)/shard_map/ppermute | solution.py:310
  42.1 1.3 %collective-permute-done.12.three_ref = bf16[2,8,2048]{2,1,0:T(8,128)(2,1)S(1)} collective-permute-done((bf16[2,8,2048]{2,1,0:T(8,128)(2,1)S(1)}, bf16[2,8,2048]{2,1,0:T(8,128)(2,1)S(1)}, u32[]{:S(2)}, u32[]{:S(2)}) %collective-permute-start.12) | collective-permute-done | bytes 65568 | tf_op jit(solution)/shard_map/ppermute | solution.py:310
  43.5 1.4 %collective-permute-done.10.one_ref = bf16[2,8,2048]{2,1,0:T(8,128)(2,1)S(1)} collective-permute-done((bf16[2,8,2048]{2,1,0:T(8,128)(2,1)S(1)}, bf16[2,8,2048]{2,1,0:T(8,128)(2,1)S(1)}, u32[]{:S(2)}, u32[]{:S(2)}) %collective-permute-start.10) | collective-permute-done | bytes 65568 | tf_op jit(solution)/shard_map/ppermute | solution.py:310
  45.0 1.1 %collective-permute-start.15 = (bf16[2,8,2048]{2,1,0:T(8,128)(2,1)S(1)}, bf16[2,8,2048]{2,1,0:T(8,128)(2,1)S(1)}, u32[]{:S(2)}, u32[]{:S(2)}) collective-permute-start(bf16[2,8,2048]{2,1,0:T(8,128)(2,1)S(1)} %owner.1.refs_0_), channel_id=1, source_target_pairs={{0,1},{1,0},{2,3},{3,2},{4,5},{5,4},{6,7},{7,6},{8,9},{9,8},{10,11... | collective-permute-start | bytes 196616 | tf_op jit(solution)/shard_map/ppermute | solution.py:310
  46.7 1.9 %collective-permute-start.13 = (bf16[2,8,2048]{2,1,0:T(8,128)(2,1)S(1)}, bf16[2,8,2048]{2,1,0:T(8,128)(2,1)S(1)}, u32[]{:S(2)}, u32[]{:S(2)}) collective-permute-start(bf16[2,8,2048]{2,1,0:T(8,128)(2,1)S(1)} %owner.1.refs_0_), channel_id=1, source_target_pairs={{0,3},{1,2},{2,1},{3,0},{4,7},{5,6},{6,5},{7,4},{8,11},{9,10},{10,... | collective-permute-start | bytes 196616 | tf_op jit(solution)/shard_map/ppermute | solution.py:310
  49.3 1.3 %collective-permute-done.14.refs_2_ = bf16[2,8,2048]{2,1,0:T(8,128)(2,1)S(1)} collective-permute-done((bf16[2,8,2048]{2,1,0:T(8,128)(2,1)S(1)}, bf16[2,8,2048]{2,1,0:T(8,128)(2,1)S(1)}, u32[]{:S(2)}, u32[]{:S(2)}) %collective-permute-start.14) | collective-permute-done | bytes 65568 | tf_op jit(solution)/shard_map/ppermute | solution.py:310
  50.7 1.2 %collective-permute-done.13.refs_1_ = bf16[2,8,2048]{2,1,0:T(8,128)(2,1)S(1)} collective-permute-done((bf16[2,8,2048]{2,1,0:T(8,128)(2,1)S(1)}, bf16[2,8,2048]{2,1,0:T(8,128)(2,1)S(1)}, u32[]{:S(2)}, u32[]{:S(2)}) %collective-permute-start.13) | collective-permute-done | bytes 65568 | tf_op jit(solution)/shard_map/ppermute | solution.py:310
  (22 shorter events, 4.4 us)
Async XLA Ops:
  0.0 5.9 %collective-permute-start = (bf16[1,8,8,128]{3,2,1,0:T(8,128)(2,1)}, bf16[1,8,8,128]{3,2,1,0:T(8,128)(2,1)S(1)}, u32[]{:S(2)}, u32[]{:S(2)}) collective-permute-start(bf16[1,8,8,128]{3,2,1,0:T(8,128)(2,1)} %queries_ref.1), channel_id=1, source_target_pairs={{0,1},{1,0},{2,3},{3,2},{4,5},{5,4},{6,7},{7,6},{8,9},{9,8},{10,11... | collective-permute-start | bytes 49160 | tf_op jit(solution)/shard_map/ppermute | solution.py:310
  5.9 8.0 %collective-permute-start.3 = (bf16[2,8,8,128]{3,2,1,0:T(8,128)(2,1)S(1)}, bf16[2,8,8,128]{3,2,1,0:T(8,128)(2,1)S(1)}, u32[]{:S(2)}, u32[]{:S(2)}) collective-permute-start(bf16[2,8,8,128]{3,2,1,0:T(8,128)(2,1)S(1)} %append.1.after_ref.refs_0_), channel_id=1, source_target_pairs={{0,6},{1,7},{2,4},{3,5},{4,2},{5,3},{6,0},{7,1},{8,14},{9,15},{10,... | collective-permute-start | bytes 98312 | tf_op jit(solution)/shard_map/ppermute | solution.py:310
  9.6 4.8 %collective-permute-start.2 = (bf16[2,8,8,128]{3,2,1,0:T(8,128)(2,1)S(1)}, bf16[2,8,8,128]{3,2,1,0:T(8,128)(2,1)S(1)}, u32[]{:S(2)}, u32[]{:S(2)}) collective-permute-start(bf16[2,8,8,128]{3,2,1,0:T(8,128)(2,1)S(1)} %append.1.after_ref.refs_0_), channel_id=1, source_target_pairs={{0,4},{1,5},{2,6},{3,7},{4,0},{5,1},{6,2},{7,3},{8,12},{9,13},{10,... | collective-permute-start | bytes 98312 | tf_op jit(solution)/shard_map/ppermute | solution.py:310
  9.6 4.8 %collective-permute-start.1 = (bf16[2,8,8,128]{3,2,1,0:T(8,128)(2,1)S(1)}, bf16[2,8,8,128]{3,2,1,0:T(8,128)(2,1)S(1)}, u32[]{:S(2)}, u32[]{:S(2)}) collective-permute-start(bf16[2,8,8,128]{3,2,1,0:T(8,128)(2,1)S(1)} %append.1.after_ref.refs_0_), channel_id=1, source_target_pairs={{0,2},{1,3},{2,0},{3,1},{4,6},{5,7},{6,4},{7,5},{8,10},{9,11},{10,... | collective-permute-start | bytes 98312 | tf_op jit(solution)/shard_map/ppermute | solution.py:310
  15.5 8.0 %collective-permute-start.5 = (bf16[2,80,128]{2,1,0:T(8,128)(2,1)S(1)}, bf16[2,80,128]{2,1,0:T(8,128)(2,1)S(1)}, u32[]{:S(2)}, u32[]{:S(2)}) collective-permute-start(bf16[2,80,128]{2,1,0:T(8,128)(2,1)S(1)} %get-tuple-element.24), channel_id=1, source_target_pairs={{0,4},{1,5},{2,6},{3,7},{4,0},{5,1},{6,2},{7,3},{8,12},{9,13},{10,... | collective-permute-start | bytes 122888 | tf_op jit(solution)/shard_map/ppermute | solution.py:310
  17.6 5.9 %collective-permute-start.6 = (bf16[2,80,128]{2,1,0:T(8,128)(2,1)S(1)}, bf16[2,80,128]{2,1,0:T(8,128)(2,1)S(1)}, u32[]{:S(2)}, u32[]{:S(2)}) collective-permute-start(bf16[2,80,128]{2,1,0:T(8,128)(2,1)S(1)} %get-tuple-element.25), channel_id=1, source_target_pairs={{0,2},{1,3},{2,0},{3,1},{4,6},{5,7},{6,4},{7,5},{8,10},{9,11},{10,... | collective-permute-start | bytes 122888 | tf_op jit(solution)/shard_map/ppermute | solution.py:310
  19.2 5.8 %collective-permute-start.4 = (bf16[2,80,128]{2,1,0:T(8,128)(2,1)S(1)}, bf16[2,80,128]{2,1,0:T(8,128)(2,1)S(1)}, u32[]{:S(2)}, u32[]{:S(2)}) collective-permute-start(bf16[2,80,128]{2,1,0:T(8,128)(2,1)S(1)} %get-tuple-element.22.after_ref), channel_id=1, source_target_pairs={{0,6},{1,7},{2,4},{3,5},{4,2},{5,3},{6,0},{7,1},{8,14},{9,15},{10,... | collective-permute-start | bytes 122888 | tf_op jit(solution)/shard_map/ppermute | solution.py:310
  25.2 3.8 %collective-permute-start.7 = (bf16[1,80,128]{2,1,0:T(8,128)(2,1)S(1)}, bf16[1,80,128]{2,1,0:T(8,128)(2,1)S(1)}, u32[]{:S(2)}, u32[]{:S(2)}) collective-permute-start(bf16[1,80,128]{2,1,0:T(8,128)(2,1)S(1)} %get-tuple-element.27.after_ref), channel_id=1, source_target_pairs={{0,1},{1,0},{2,3},{3,2},{4,5},{5,4},{6,7},{7,6},{8,9},{9,8},{10,11... | collective-permute-start | bytes 61448 | tf_op jit(solution)/shard_map/ppermute | solution.py:310
  31.5 5.9 %collective-permute-start.8 = (bf16[4,8,2048]{2,1,0:T(8,128)(2,1)S(1)}, bf16[4,8,2048]{2,1,0:T(8,128)(2,1)S(1)}, u32[]{:S(2)}, u32[]{:S(2)}) collective-permute-start(bf16[4,8,2048]{2,1,0:T(8,128)(2,1)S(1)} %get-tuple-element.30), channel_id=1, source_target_pairs={{0,1},{1,0},{2,3},{3,2},{4,5},{5,4},{6,7},{7,6},{8,9},{9,8},{10,11... | collective-permute-start | bytes 393224 | tf_op jit(solution)/shard_map/ppermute | solution.py:310
  32.5 4.9 %copy-start = (bf16[1,8,2048]{2,1,0:T(8,128)(2,1)S(1)}, bf16[1,8,2048]{2,1,0:T(8,128)(2,1)}, u32[]{:S(2)}) copy-start(bf16[1,8,2048]{2,1,0:T(8,128)(2,1)} %residual_ref.1) | copy-start | bytes 98308
  37.5 4.7 %collective-permute-start.11 = (bf16[2,8,2048]{2,1,0:T(8,128)(2,1)S(1)}, bf16[2,8,2048]{2,1,0:T(8,128)(2,1)S(1)}, u32[]{:S(2)}, u32[]{:S(2)}) collective-permute-start(bf16[2,8,2048]{2,1,0:T(8,128)(2,1)S(1)} %get-tuple-element.31), channel_id=1, source_target_pairs={{0,12},{1,13},{2,14},{3,15},{4,8},{5,9},{6,10},{7,11},{8,4},{9,5},... | collective-permute-start | bytes 196616 | tf_op jit(solution)/shard_map/ppermute | solution.py:310
  37.6 4.6 %collective-permute-start.9 = (bf16[2,8,2048]{2,1,0:T(8,128)(2,1)S(1)}, bf16[2,8,2048]{2,1,0:T(8,128)(2,1)S(1)}, u32[]{:S(2)}, u32[]{:S(2)}) collective-permute-start(bf16[2,8,2048]{2,1,0:T(8,128)(2,1)S(1)} %get-tuple-element.31), channel_id=1, source_target_pairs={{0,8},{1,9},{2,10},{3,11},{4,12},{5,13},{6,14},{7,15},{8,0},{9,1},... | collective-permute-start | bytes 196616 | tf_op jit(solution)/shard_map/ppermute | solution.py:310
  37.6 5.8 %collective-permute-start.12 = (bf16[2,8,2048]{2,1,0:T(8,128)(2,1)S(1)}, bf16[2,8,2048]{2,1,0:T(8,128)(2,1)S(1)}, u32[]{:S(2)}, u32[]{:S(2)}) collective-permute-start(bf16[2,8,2048]{2,1,0:T(8,128)(2,1)S(1)} %get-tuple-element.32), channel_id=1, source_target_pairs={{0,14},{1,15},{2,12},{3,13},{4,10},{5,11},{6,8},{7,9},{8,6},{9,7},... | collective-permute-start | bytes 196616 | tf_op jit(solution)/shard_map/ppermute | solution.py:310
  39.3 5.6 %collective-permute-start.10 = (bf16[2,8,2048]{2,1,0:T(8,128)(2,1)S(1)}, bf16[2,8,2048]{2,1,0:T(8,128)(2,1)S(1)}, u32[]{:S(2)}, u32[]{:S(2)}) collective-permute-start(bf16[2,8,2048]{2,1,0:T(8,128)(2,1)S(1)} %get-tuple-element.32), channel_id=1, source_target_pairs={{0,10},{1,11},{2,8},{3,9},{4,14},{5,15},{6,12},{7,13},{8,2},{9,3},... | collective-permute-start | bytes 196616 | tf_op jit(solution)/shard_map/ppermute | solution.py:310
  45.0 4.3 %collective-permute-start.15 = (bf16[2,8,2048]{2,1,0:T(8,128)(2,1)S(1)}, bf16[2,8,2048]{2,1,0:T(8,128)(2,1)S(1)}, u32[]{:S(2)}, u32[]{:S(2)}) collective-permute-start(bf16[2,8,2048]{2,1,0:T(8,128)(2,1)S(1)} %owner.1.refs_0_), channel_id=1, source_target_pairs={{0,1},{1,0},{2,3},{3,2},{4,5},{5,4},{6,7},{7,6},{8,9},{9,8},{10,11... | collective-permute-start | bytes 196616 | tf_op jit(solution)/shard_map/ppermute | solution.py:310
  46.1 4.5 %collective-permute-start.14 = (bf16[2,8,2048]{2,1,0:T(8,128)(2,1)S(1)}, bf16[2,8,2048]{2,1,0:T(8,128)(2,1)S(1)}, u32[]{:S(2)}, u32[]{:S(2)}) collective-permute-start(bf16[2,8,2048]{2,1,0:T(8,128)(2,1)S(1)} %owner.1.refs_0_), channel_id=1, source_target_pairs={{0,2},{1,3},{2,0},{3,1},{4,6},{5,7},{6,4},{7,5},{8,10},{9,11},{10,... | collective-permute-start | bytes 196616 | tf_op jit(solution)/shard_map/ppermute | solution.py:310
  46.7 5.2 %collective-permute-start.13 = (bf16[2,8,2048]{2,1,0:T(8,128)(2,1)S(1)}, bf16[2,8,2048]{2,1,0:T(8,128)(2,1)S(1)}, u32[]{:S(2)}, u32[]{:S(2)}) collective-permute-start(bf16[2,8,2048]{2,1,0:T(8,128)(2,1)S(1)} %owner.1.refs_0_), channel_id=1, source_target_pairs={{0,3},{1,2},{2,1},{3,0},{4,7},{5,6},{6,5},{7,4},{8,11},{9,10},{10,... | collective-permute-start | bytes 196616 | tf_op jit(solution)/shard_map/ppermute | solution.py:310

commit v2 on v1

--- a/solution.py
+++ b/solution.py
@@ -25,26 +25,22 @@
     return high, middle, rest - middle
 
 
-def weight_copies(slots, weight_ref, held_ref, sems, cuts=1):
+def weight_copies(units, weight_ref, held_ref, sems):
     rank = lax.axis_index("tp")
-    width = held_ref.shape[2]
-    piece = width // cuts
+    columns = held_ref.shape[2]
     copies = []
-    for i, slot in enumerate(slots):
-        for c in range(cuts):
-            start = pl.multiple_of((rank ^ slot) * width + c * piece, piece)
-            copies.append(
-                pltpu.make_async_copy(
-                    weight_ref.at[0, :, pl.ds(start, piece)],
-                    held_ref.at[i, :, c * piece : (c + 1) * piece],
-                    sems.at[i * cuts + c],
-                )
+    for i, (slot, half) in enumerate(units):
+        start = pl.multiple_of(((rank ^ slot) * 2 + half) * columns, columns)
+        copies.append(
+            pltpu.make_async_copy(
+                weight_ref.at[0, :, pl.ds(start, columns)], held_ref.at[i], sems.at[i]
             )
+        )
     return copies
 
 
 def stage_cache_kernel(
-    per, slots, lengths_ref, new_ref, kv_ref, queries_ref, weight_ref,
+    per, units, lengths_ref, new_ref, kv_ref, queries_ref, weight_ref,
     stored_ref, limit_ref, near_ref, held_ref, lengths, new, kv, sems, held_sems,
 ):
     rank = lax.axis_index("tp")
@@ -55,7 +51,7 @@
         pltpu.make_async_copy(kv_ref.at[0], kv, sems.at[2]),
         pltpu.make_async_copy(queries_ref, near_ref, sems.at[3]),
     ]
-    held = weight_copies(slots, weight_ref, held_ref, held_sems)
+    held = weight_copies(units, weight_ref, held_ref, held_sems)
     for copy in copies + held:
         copy.start()
     for copy in copies:
@@ -82,9 +78,9 @@
         copy.wait()
 
 
-def stage_kernel(slots, weight_ref, after_ref, held_ref, sems):
+def stage_kernel(units, weight_ref, after_ref, held_ref, sems):
     del after_ref
-    copies = weight_copies(slots, weight_ref, held_ref, sems)
+    copies = weight_copies(units, weight_ref, held_ref, sems)
     for copy in copies:
         copy.start()
     for copy in copies:
@@ -210,6 +206,12 @@
             out_ref[i, :, at : at + QB] = block.astype(out_ref.dtype)
 
 
+def project_units(flat, held, places, out_ref):
+    for i, (array, index) in enumerate(places):
+        columns = held[array].shape[2]
+        project_columns(flat, held[array].at[index], out_ref, i // 2, i % 2 * columns)
+
+
 def project_away_kernel(rows, heads, places, kept_ref, got_ref, *refs):
     held, (flat_ref, out_ref) = refs[:-2], refs[-2:]
     mixed, _, total = merged([kept_ref[0], got_ref[0]])
@@ -218,25 +220,11 @@
         [attended[h * rows : (h + 1) * rows] for h in range(heads)], axis=1
     ).astype(BF16)
     flat_ref[...] = flat
-    for i, (array, index) in enumerate(places):
-        project_columns(flat, held[array].at[index], out_ref, i, 0)
-
-
-def project_own_kernel(places, slots, cuts, flat_ref, weight_ref, *refs):
-    held, (out_ref, late_ref, sems) = refs[:-3], refs[-3:]
-    copies = weight_copies(slots, weight_ref, late_ref, sems, cuts)
-    for copy in copies:
-        copy.start()
-    flat = flat_ref[...]
-    for i, place in enumerate(places):
-        if place is not None:
-            project_columns(flat, held[place[0]].at[place[1]], out_ref, i, 0)
-    piece = late_ref.shape[2] // cuts
-    for late, slot in enumerate(slots):
-        for c in range(cuts):
-            copies[late * cuts + c].wait()
-            columns = late_ref.at[late, :, c * piece : (c + 1) * piece]
-            project_columns(flat, columns, out_ref, slot >> 1, c * piece)
+    project_units(flat, held, places, out_ref)
+
+
+def project_own_kernel(places, flat_ref, *refs):
+    project_units(flat_ref[...], refs[:-1], places, refs[-1])
 
 
 def split_kernel(kept_ref, got_ref, send_ref, keep_ref):
@@ -312,38 +300,41 @@
     weight = in_hbm(out_weight)
     quarter = tp // 4
     groups = [g * quarter for g in range(1, 4)]
-    order = list(range(1, tp, 2)) + list(range(0, tp, 2))
+    order = [(slot, h) for slot in (*range(1, tp, 2), *range(0, tp, 2)) for h in range(2)]
     each = tp // 8
     staged = []
 
-    def next_slots(count):
-        used = sum(len(slots) for slots, _ in staged)
+    def next_units(count):
+        used = sum(len(units) for units, _ in staged)
         return order[used : used + count * each]
 
+    def held_shape(units):
+        return pltpu.VMEM((len(units), depth, width // 2), BF16)
+
     def stage(after, count):
-        slots = next_slots(count)
+        units = next_units(count)
         held = call(
-            functools.partial(stage_kernel, slots),
+            functools.partial(stage_kernel, units),
             "stage",
-            pltpu.VMEM((len(slots), depth, width), BF16),
+            held_shape(units),
             (weight, after),
             in_specs=[ANY_SPEC, VMEM_SPEC],
-            scratch=[pltpu.SemaphoreType.DMA((len(slots),))],
-            cost=4 * MIB * count,
-        )
-        staged.append((slots, held))
+            scratch=[pltpu.SemaphoreType.DMA((len(units),))],
+            cost=2 * MIB * count,
+        )
+        staged.append((units, held))
         return held
 
     got = exchanged(queries, 1)
-    slots = next_slots(1)
+    units = next_units(2)
     stored, limit, have, held = call(
-        functools.partial(stage_cache_kernel, tp // kv_heads, slots),
+        functools.partial(stage_cache_kernel, tp // kv_heads, units),
         "stage_cache",
         [
             pltpu.VMEM(kv_cache.shape[1:], BF16),
             pltpu.VMEM((rows, span), jnp.int32),
             pltpu.VMEM(queries.shape, BF16),
-            pltpu.VMEM((len(slots), depth, width), BF16),
+            held_shape(units),
         ],
         (in_hbm(lengths), in_hbm(new_kv), in_hbm(kv_cache), in_hbm(queries), weight),
         in_specs=[ANY_SPEC] * 5,
@@ -352,11 +343,11 @@
             pltpu.VMEM(new_kv.shape[1:], BF16),
             pltpu.VMEM(kv_cache.shape[1:], BF16),
             pltpu.SemaphoreType.DMA((4,)),
-            pltpu.SemaphoreType.DMA((len(slots),)),
+            pltpu.SemaphoreType.DMA((len(units),)),
         ],
         cost=8 * MIB,
     )
-    staged.append((slots, held))
+    staged.append((units, held))
     after = limit
     for b in range(bits - 2):
         count = 2 << b
@@ -368,7 +359,7 @@
             got = exchanged(have, 2 << b)
     all_queries = [have, *(exchanged(have, k) for k in reversed(groups))]
     all_queries[1:] = all_queries[:0:-1]
-    after = stage(have, 2)
+    after = stage(have, 5)
     packed_block = (heads * rows + STAT_ROWS, dim)
     partial = call(
         attention_kernel,
@@ -378,26 +369,23 @@
         scratch=[pltpu.VMEM((heads * tp, rows, span), F32)] * 2,
         cost=8 * MIB,
     )
-    pending = [partial[0], *(exchanged(partial[g], g * quarter) for g in (3, 2, 1))]
-    after = stage(partial[3], 2)
+    pending = [partial[0], *(exchanged(partial[g], g * quarter) for g in (1, 2, 3))]
+    after = stage(partial[3], 6)
     for b in reversed(range(bits - 2)):
         send, kept = call(
             merge_kernel, "merge", [struct((1 << b, *packed_block), BF16)] * 2, (after, *pending)
         )
         pending = [kept, exchanged(send, 1 << b)]
         after = send
-    stage(send, 1)
+    stage(send, 3)
 
     where = {
-        slot: (array, i) for array, (slots, _) in enumerate(staged) for i, slot in enumerate(slots)
+        unit: (array, i) for array, (units, _) in enumerate(staged) for i, unit in enumerate(units)
     }
-    late = next_slots(tp)
+    places = [where[unit] for unit in order]
     held = [array for _, array in staged]
-    cuts = max(1, width // 512)
     flat, away = call(
-        functools.partial(
-            project_away_kernel, rows, heads, [where[slot] for slot in range(1, tp, 2)]
-        ),
+        functools.partial(project_away_kernel, rows, heads, places[:tp]),
         "project_away",
         [struct((rows, depth), BF16), struct((half, rows, width), BF16)],
         (*pending, *held),
@@ -405,18 +393,10 @@
     )
     got = exchanged(away, 1)
     kept = call(
-        functools.partial(
-            project_own_kernel, [where.get(slot) for slot in range(0, tp, 2)], late, cuts
-        ),
+        functools.partial(project_own_kernel, places[tp:]),
         "project_own",
         struct((half, rows, width), F32),
-        (flat, weight, *held),
-        in_specs=[VMEM_SPEC, ANY_SPEC] + [VMEM_SPEC] * len(held),
-        scratch=[
-            pltpu.VMEM((len(late), depth, width), BF16),
-            pltpu.SemaphoreType.DMA((len(late) * cuts,)),
-        ],
-        mib=14,
+        (flat, *held),
         cost=16 * MIB,
     )
     for b in range(1, bits - 2):
@@ -439,7 +419,7 @@
         owner_kernel, "owner", struct((2, rows, width), BF16), (near, one, two, three)
     )
     high = 1 << (bits - 1)
-    parts = [(0, own)] + [(k, exchanged(own, k)) for k in reversed(range(1, high))]
+    parts = [(0, own)] + [(k, exchanged(own, k)) for k in range(1, high)]
     return call(
         functools.partial(place_kernel, [offset for offset, _ in parts], high),
         "placed",

time: 52.7 us -> 53.4 us (1.013)
  transfers between devices with their start and end apart: 16 -> 16, of which waited for: 9 -> 8; matrix products, arithmetic and copies ran while one was open for 0% -> 0% of each run, Pallas kernels for 32% -> 32%
where the time goes in v2:
time: 53.4 us; the launch traced here: 53.3 us
  Pallas kernels  21.7 us (41%)
  starting transfers between devices  21 us (39%)
  waiting for transfers between devices  10.4 us (19%)
    pallas_call x12, Pallas kernels, call(): pl.pallas_call(kernel, out_shape=outs, in_specs=in_specs or [VMEM_SPEC] *...  21.7 us
    ppermute x16, starting transfers between devices, exchanged(): return lax.ppermute(array, ('section', 'tp'), pairs)  21 us
    ppermute x16, waiting for transfers between devices, exchanged(): return lax.ppermute(array, ('section', 'tp'), pairs)  10.4 us
  transfers between devices with their start and end apart: 16, of which 8 were waited for; matrix products, arithmetic and copies ran while one was open for 0% of the time, Pallas kernels for 32%

profile of v2, /device:TPU:0, one launch (start us, length us, event | category | flops | bytes accessed | tf_op | source)
XLA Modules:
  0.0 53.3 jit_solution(11927552319801687072)
XLA Ops:
  0.0 3.0 %collective-permute-start = (bf16[1,8,8,128]{3,2,1,0:T(8,128)(2,1)}, bf16[1,8,8,128]{3,2,1,0:T(8,128)(2,1)S(1)}, u32[]{:S(2)}, u32[]{:S(2)}) collective-permute-start(bf16[1,8,8,128]{3,2,1,0:T(8,128)(2,1)} %queries_ref.1), channel_id=1, source_target_pairs={{0,1},{1,0},{2,3},{3,2},{4,5},{5,4},{6,7},{7,6},{8,9},{9,8},{10,11... | collective-permute-start | bytes 49160 | tf_op jit(solution)/shard_map/ppermute | solution.py:298
  3.0 2.9 %stage_cache.1 = (bf16[8,2,4,128,128]{4,3,2,1,0:T(8,128)(2,1)S(1)}, s32[8,128]{1,0:T(8,128)S(1)}, bf16[1,8,8,128]{3,2,1,0:T(8,128)(2,1)S(1)}, bf16[2,1024,1024]{2,1,0:T(8,128)(2,1)S(1)}) custom-call(s32[1,8]{1,0:T(1,128)} %lengths_ref.1, bf16[1,8,2,4,128]{4,3,2,1,0:T(4,128)(2,1)} %new_ref.1, bf16[1,8,2,4,128,128]{5,4,3,2,1,0:T(8,128)(2,1)} %kv_ref.1, ...), custom_call_target="tpu_custom_call" | custom-call | flops 8388608 | bytes 8388608 | tf_op jit(solution)/shard_map/stage_cache/pallas_call | solution.py:267
  5.9 3.7 %collective-permute-start.3 = (bf16[2,8,8,128]{3,2,1,0:T(8,128)(2,1)S(1)}, bf16[2,8,8,128]{3,2,1,0:T(8,128)(2,1)S(1)}, u32[]{:S(2)}, u32[]{:S(2)}) collective-permute-start(bf16[2,8,8,128]{3,2,1,0:T(8,128)(2,1)S(1)} %append.1.after_ref.refs_0_), channel_id=1, source_target_pairs={{0,6},{1,7},{2,4},{3,5},{4,2},{5,3},{6,0},{7,1},{8,14},{9,15},{10,... | collective-permute-start | bytes 98312 | tf_op jit(solution)/shard_map/ppermute | solution.py:298
  9.6 0.8 %collective-permute-start.1 = (bf16[2,8,8,128]{3,2,1,0:T(8,128)(2,1)S(1)}, bf16[2,8,8,128]{3,2,1,0:T(8,128)(2,1)S(1)}, u32[]{:S(2)}, u32[]{:S(2)}) collective-permute-start(bf16[2,8,8,128]{3,2,1,0:T(8,128)(2,1)S(1)} %append.1.after_ref.refs_0_), channel_id=1, source_target_pairs={{0,2},{1,3},{2,0},{3,1},{4,6},{5,7},{6,4},{7,5},{8,10},{9,11},{10,... | collective-permute-start | bytes 98312 | tf_op jit(solution)/shard_map/ppermute | solution.py:298
  10.4 4.1 %stage.3.after_ref.refs_1_ = bf16[5,1024,1024]{2,1,0:T(8,128)(2,1)S(1)} custom-call(bf16[1,1024,16384]{2,1,0:T(8,128)(2,1)} %weight_ref.7, bf16[2,8,8,128]{3,2,1,0:T(8,128)(2,1)S(1)} %append.1.after_ref.refs_0_), custom_call_target="tpu_custom_call" | custom-call | flops 10485760 | bytes 10485760 | tf_op jit(solution)/shard_map/stage/pallas_call | solution.py:267
  14.6 1.1 %attention.1 = (bf16[2,80,128]{2,1,0:T(8,128)(2,1)S(1)}, bf16[2,80,128]{2,1,0:T(8,128)(2,1)S(1)}, bf16[2,80,128]{2,1,0:T(8,128)(2,1)S(1)}, bf16[2,80,128]{2,1,0:T(8,128)(2,1)S(1)}) custom-call(bf16[8,2,4,128,128]{4,3,2,1,0:T(8,128)(2,1)S(1)} %get-tuple-element.19.stored_ref, s32[8,128]{1,0:T(8,128)S(1)} %get-tuple-element.20.after_ref.limit_ref, ...), custom_call_target="tpu_custom_call" | custom-call | flops 8388608 | bytes 8388608 | tf_op jit(solution)/shard_map/attention/pallas_call | solution.py:267
  15.7 1.3 %collective-permute-start.4 = (bf16[2,80,128]{2,1,0:T(8,128)(2,1)S(1)}, bf16[2,80,128]{2,1,0:T(8,128)(2,1)S(1)}, u32[]{:S(2)}, u32[]{:S(2)}) collective-permute-start(bf16[2,80,128]{2,1,0:T(8,128)(2,1)S(1)} %get-tuple-element.24), channel_id=1, source_target_pairs={{0,2},{1,3},{2,0},{3,1},{4,6},{5,7},{6,4},{7,5},{8,10},{9,11},{10,... | collective-permute-start | bytes 122888 | tf_op jit(solution)/shard_map/ppermute | solution.py:298
  17.0 2.9 %collective-permute-start.5 = (bf16[2,80,128]{2,1,0:T(8,128)(2,1)S(1)}, bf16[2,80,128]{2,1,0:T(8,128)(2,1)S(1)}, u32[]{:S(2)}, u32[]{:S(2)}) collective-permute-start(bf16[2,80,128]{2,1,0:T(8,128)(2,1)S(1)} %get-tuple-element.25), channel_id=1, source_target_pairs={{0,4},{1,5},{2,6},{3,7},{4,0},{5,1},{6,2},{7,3},{8,12},{9,13},{10,... | collective-permute-start | bytes 122888 | tf_op jit(solution)/shard_map/ppermute | solution.py:298
  20.1 4.8 %stage.4.after_ref.refs_2_ = bf16[6,1024,1024]{2,1,0:T(8,128)(2,1)S(1)} custom-call(bf16[1,1024,16384]{2,1,0:T(8,128)(2,1)} %weight_ref.7, bf16[2,80,128]{2,1,0:T(8,128)(2,1)S(1)} %get-tuple-element.22.after_ref), custom_call_target="tpu_custom_call" | custom-call | flops 12582912 | bytes 12582912 | tf_op jit(solution)/shard_map/stage/pallas_call | solution.py:267
  24.9 0.8 %collective-permute-done.6.refs_3_ = bf16[2,80,128]{2,1,0:T(8,128)(2,1)S(1)} collective-permute-done((bf16[2,80,128]{2,1,0:T(8,128)(2,1)S(1)}, bf16[2,80,128]{2,1,0:T(8,128)(2,1)S(1)}, u32[]{:S(2)}, u32[]{:S(2)}) %collective-permute-start.6) | collective-permute-done | bytes 40992 | tf_op jit(solution)/shard_map/ppermute | solution.py:298
  25.9 1.0 %collective-permute-start.7 = (bf16[1,80,128]{2,1,0:T(8,128)(2,1)S(1)}, bf16[1,80,128]{2,1,0:T(8,128)(2,1)S(1)}, u32[]{:S(2)}, u32[]{:S(2)}) collective-permute-start(bf16[1,80,128]{2,1,0:T(8,128)(2,1)S(1)} %get-tuple-element.27.after_ref), channel_id=1, source_target_pairs={{0,1},{1,0},{2,3},{3,2},{4,5},{5,4},{6,7},{7,6},{8,9},{9,8},{10,11... | collective-permute-start | bytes 61448 | tf_op jit(solution)/shard_map/ppermute | solution.py:298
  26.8 2.9 %stage.5.refs_3_ = bf16[3,1024,1024]{2,1,0:T(8,128)(2,1)S(1)} custom-call(bf16[1,1024,16384]{2,1,0:T(8,128)(2,1)} %weight_ref.7, bf16[1,80,128]{2,1,0:T(8,128)(2,1)S(1)} %get-tuple-element.27.after_ref), custom_call_target="tpu_custom_call" | custom-call | flops 6291456 | bytes 6291456 | tf_op jit(solution)/shard_map/stage/pallas_call | solution.py:267
  29.8 2.5 %project_away.1 = (bf16[8,1024]{1,0:T(8,128)(2,1)S(1)}, bf16[4,8,2048]{2,1,0:T(8,128)(2,1)S(1)}) custom-call(bf16[1,80,128]{2,1,0:T(8,128)(2,1)S(1)} %get-tuple-element.26.kept_ref, bf16[1,80,128]{2,1,0:T(8,128)(2,1)S(1)} %collective-permute-done.7.got_ref, bf16[2,1024,1024]{2,1,0:T(8,128)(2,1)S(1)} %get-tuple-element.28.refs_0_, ...), custom_call_target="tpu_custom_call" | custom-call | flops 16777216 | bytes 16777216 | tf_op jit(solution)/shard_map/project_away/pallas_call | solution.py:267
  32.2 1.2 %collective-permute-start.8 = (bf16[4,8,2048]{2,1,0:T(8,128)(2,1)S(1)}, bf16[4,8,2048]{2,1,0:T(8,128)(2,1)S(1)}, u32[]{:S(2)}, u32[]{:S(2)}) collective-permute-start(bf16[4,8,2048]{2,1,0:T(8,128)(2,1)S(1)} %get-tuple-element.30), channel_id=1, source_target_pairs={{0,1},{1,0},{2,3},{3,2},{4,5},{5,4},{6,7},{7,6},{8,9},{9,8},{10,11... | collective-permute-start | bytes 393224 | tf_op jit(solution)/shard_map/ppermute | solution.py:298
  33.4 2.4 %project_own.1.kept_ref = f32[4,8,2048]{2,1,0:T(8,128)S(1)} custom-call(bf16[8,1024]{1,0:T(8,128)(2,1)S(1)} %get-tuple-element.29.flat_ref, bf16[2,1024,1024]{2,1,0:T(8,128)(2,1)S(1)} %get-tuple-element.28.refs_0_, bf16[5,1024,1024]{2,1,0:T(8,128)(2,1)S(1)} %stage.3.after_ref.refs_1_, bf16[6,1024,1024]{2,1,0:T(8,128)(2,1)S(1)} %stage.4.after_ref.refs_2_, ...), custom_call_target="tpu_custom_call" | custom-call | flops 16777216 | bytes 16777216 | tf_op jit(solution)/shard_map/project_own/pallas_call | solution.py:267
  35.8 1.5 %collective-permute-done.8.got_ref = bf16[4,8,2048]{2,1,0:T(8,128)(2,1)S(1)} collective-permute-done((bf16[4,8,2048]{2,1,0:T(8,128)(2,1)S(1)}, bf16[4,8,2048]{2,1,0:T(8,128)(2,1)S(1)}, u32[]{:S(2)}, u32[]{:S(2)}) %collective-permute-start.8) | collective-permute-done | bytes 131104 | tf_op jit(solution)/shard_map/ppermute | solution.py:298
  38.0 2.4 %collective-permute-start.12 = (bf16[2,8,2048]{2,1,0:T(8,128)(2,1)S(1)}, bf16[2,8,2048]{2,1,0:T(8,128)(2,1)S(1)}, u32[]{:S(2)}, u32[]{:S(2)}) collective-permute-start(bf16[2,8,2048]{2,1,0:T(8,128)(2,1)S(1)} %get-tuple-element.32), channel_id=1, source_target_pairs={{0,14},{1,15},{2,12},{3,13},{4,10},{5,11},{6,8},{7,9},{8,6},{9,7},... | collective-permute-start | bytes 196616 | tf_op jit(solution)/shard_map/ppermute | solution.py:298
  40.7 2.0 %collective-permute-done.11.two_ref = bf16[2,8,2048]{2,1,0:T(8,128)(2,1)S(1)} collective-permute-done((bf16[2,8,2048]{2,1,0:T(8,128)(2,1)S(1)}, bf16[2,8,2048]{2,1,0:T(8,128)(2,1)S(1)}, u32[]{:S(2)}, u32[]{:S(2)}) %collective-permute-start.11) | collective-permute-done | bytes 65568 | tf_op jit(solution)/shard_map/ppermute | solution.py:298
  42.7 1.5 %collective-permute-done.12.three_ref = bf16[2,8,2048]{2,1,0:T(8,128)(2,1)S(1)} collective-permute-done((bf16[2,8,2048]{2,1,0:T(8,128)(2,1)S(1)}, bf16[2,8,2048]{2,1,0:T(8,128)(2,1)S(1)}, u32[]{:S(2)}, u32[]{:S(2)}) %collective-permute-start.12) | collective-permute-done | bytes 65568 | tf_op jit(solution)/shard_map/ppermute | solution.py:298
  44.1 1.4 %collective-permute-done.10.one_ref = bf16[2,8,2048]{2,1,0:T(8,128)(2,1)S(1)} collective-permute-done((bf16[2,8,2048]{2,1,0:T(8,128)(2,1)S(1)}, bf16[2,8,2048]{2,1,0:T(8,128)(2,1)S(1)}, u32[]{:S(2)}, u32[]{:S(2)}) %collective-permute-start.10) | collective-permute-done | bytes 65568 | tf_op jit(solution)/shard_map/ppermute | solution.py:298
  45.7 1.3 %collective-permute-start.15 = (bf16[2,8,2048]{2,1,0:T(8,128)(2,1)S(1)}, bf16[2,8,2048]{2,1,0:T(8,128)(2,1)S(1)}, u32[]{:S(2)}, u32[]{:S(2)}) collective-permute-start(bf16[2,8,2048]{2,1,0:T(8,128)(2,1)S(1)} %owner.1.refs_0_), channel_id=1, source_target_pairs={{0,3},{1,2},{2,1},{3,0},{4,7},{5,6},{6,5},{7,4},{8,11},{9,10},{10,... | collective-permute-start | bytes 196616 | tf_op jit(solution)/shard_map/ppermute | solution.py:298
  46.9 1.4 %collective-permute-start.14 = (bf16[2,8,2048]{2,1,0:T(8,128)(2,1)S(1)}, bf16[2,8,2048]{2,1,0:T(8,128)(2,1)S(1)}, u32[]{:S(2)}, u32[]{:S(2)}) collective-permute-start(bf16[2,8,2048]{2,1,0:T(8,128)(2,1)S(1)} %owner.1.refs_0_), channel_id=1, source_target_pairs={{0,2},{1,3},{2,0},{3,1},{4,6},{5,7},{6,4},{7,5},{8,10},{9,11},{10,... | collective-permute-start | bytes 196616 | tf_op jit(solution)/shard_map/ppermute | solution.py:298
  48.3 0.9 %collective-permute-start.13 = (bf16[2,8,2048]{2,1,0:T(8,128)(2,1)S(1)}, bf16[2,8,2048]{2,1,0:T(8,128)(2,1)S(1)}, u32[]{:S(2)}, u32[]{:S(2)}) collective-permute-start(bf16[2,8,2048]{2,1,0:T(8,128)(2,1)S(1)} %owner.1.refs_0_), channel_id=1, source_target_pairs={{0,1},{1,0},{2,3},{3,2},{4,5},{5,4},{6,7},{7,6},{8,9},{9,8},{10,11... | collective-permute-start | bytes 196616 | tf_op jit(solution)/shard_map/ppermute | solution.py:298
  49.2 2.3 %collective-permute-done.15.refs_3_ = bf16[2,8,2048]{2,1,0:T(8,128)(2,1)S(1)} collective-permute-done((bf16[2,8,2048]{2,1,0:T(8,128)(2,1)S(1)}, bf16[2,8,2048]{2,1,0:T(8,128)(2,1)S(1)}, u32[]{:S(2)}, u32[]{:S(2)}) %collective-permute-start.15) | collective-permute-done | bytes 65568 | tf_op jit(solution)/shard_map/ppermute | solution.py:298
  (22 shorter events, 3.3 us)
Async XLA Ops:
  0.0 5.9 %collective-permute-start = (bf16[1,8,8,128]{3,2,1,0:T(8,128)(2,1)}, bf16[1,8,8,128]{3,2,1,0:T(8,128)(2,1)S(1)}, u32[]{:S(2)}, u32[]{:S(2)}) collective-permute-start(bf16[1,8,8,128]{3,2,1,0:T(8,128)(2,1)} %queries_ref.1), channel_id=1, source_target_pairs={{0,1},{1,0},{2,3},{3,2},{4,5},{5,4},{6,7},{7,6},{8,9},{9,8},{10,11... | collective-permute-start | bytes 49160 | tf_op jit(solution)/shard_map/ppermute | solution.py:298
  5.9 8.6 %collective-permute-start.3 = (bf16[2,8,8,128]{3,2,1,0:T(8,128)(2,1)S(1)}, bf16[2,8,8,128]{3,2,1,0:T(8,128)(2,1)S(1)}, u32[]{:S(2)}, u32[]{:S(2)}) collective-permute-start(bf16[2,8,8,128]{3,2,1,0:T(8,128)(2,1)S(1)} %append.1.after_ref.refs_0_), channel_id=1, source_target_pairs={{0,6},{1,7},{2,4},{3,5},{4,2},{5,3},{6,0},{7,1},{8,14},{9,15},{10,... | collective-permute-start | bytes 98312 | tf_op jit(solution)/shard_map/ppermute | solution.py:298
  9.6 4.9 %collective-permute-start.2 = (bf16[2,8,8,128]{3,2,1,0:T(8,128)(2,1)S(1)}, bf16[2,8,8,128]{3,2,1,0:T(8,128)(2,1)S(1)}, u32[]{:S(2)}, u32[]{:S(2)}) collective-permute-start(bf16[2,8,8,128]{3,2,1,0:T(8,128)(2,1)S(1)} %append.1.after_ref.refs_0_), channel_id=1, source_target_pairs={{0,4},{1,5},{2,6},{3,7},{4,0},{5,1},{6,2},{7,3},{8,12},{9,13},{10,... | collective-permute-start | bytes 98312 | tf_op jit(solution)/shard_map/ppermute | solution.py:298
  9.6 5.0 %collective-permute-start.1 = (bf16[2,8,8,128]{3,2,1,0:T(8,128)(2,1)S(1)}, bf16[2,8,8,128]{3,2,1,0:T(8,128)(2,1)S(1)}, u32[]{:S(2)}, u32[]{:S(2)}) collective-permute-start(bf16[2,8,8,128]{3,2,1,0:T(8,128)(2,1)S(1)} %append.1.after_ref.refs_0_), channel_id=1, source_target_pairs={{0,2},{1,3},{2,0},{3,1},{4,6},{5,7},{6,4},{7,5},{8,10},{9,11},{10,... | collective-permute-start | bytes 98312 | tf_op jit(solution)/shard_map/ppermute | solution.py:298
  15.7 9.2 %collective-permute-start.4 = (bf16[2,80,128]{2,1,0:T(8,128)(2,1)S(1)}, bf16[2,80,128]{2,1,0:T(8,128)(2,1)S(1)}, u32[]{:S(2)}, u32[]{:S(2)}) collective-permute-start(bf16[2,80,128]{2,1,0:T(8,128)(2,1)S(1)} %get-tuple-element.24), channel_id=1, source_target_pairs={{0,2},{1,3},{2,0},{3,1},{4,6},{5,7},{6,4},{7,5},{8,10},{9,11},{10,... | collective-permute-start | bytes 122888 | tf_op jit(solution)/shard_map/ppermute | solution.py:298
  17.0 7.9 %collective-permute-start.5 = (bf16[2,80,128]{2,1,0:T(8,128)(2,1)S(1)}, bf16[2,80,128]{2,1,0:T(8,128)(2,1)S(1)}, u32[]{:S(2)}, u32[]{:S(2)}) collective-permute-start(bf16[2,80,128]{2,1,0:T(8,128)(2,1)S(1)} %get-tuple-element.25), channel_id=1, source_target_pairs={{0,4},{1,5},{2,6},{3,7},{4,0},{5,1},{6,2},{7,3},{8,12},{9,13},{10,... | collective-permute-start | bytes 122888 | tf_op jit(solution)/shard_map/ppermute | solution.py:298
  19.9 5.8 %collective-permute-start.6 = (bf16[2,80,128]{2,1,0:T(8,128)(2,1)S(1)}, bf16[2,80,128]{2,1,0:T(8,128)(2,1)S(1)}, u32[]{:S(2)}, u32[]{:S(2)}) collective-permute-start(bf16[2,80,128]{2,1,0:T(8,128)(2,1)S(1)} %get-tuple-element.22.after_ref), channel_id=1, source_target_pairs={{0,6},{1,7},{2,4},{3,5},{4,2},{5,3},{6,0},{7,1},{8,14},{9,15},{10,... | collective-permute-start | bytes 122888 | tf_op jit(solution)/shard_map/ppermute | solution.py:298
  25.9 3.9 %collective-permute-start.7 = (bf16[1,80,128]{2,1,0:T(8,128)(2,1)S(1)}, bf16[1,80,128]{2,1,0:T(8,128)(2,1)S(1)}, u32[]{:S(2)}, u32[]{:S(2)}) collective-permute-start(bf16[1,80,128]{2,1,0:T(8,128)(2,1)S(1)} %get-tuple-element.27.after_ref), channel_id=1, source_target_pairs={{0,1},{1,0},{2,3},{3,2},{4,5},{5,4},{6,7},{7,6},{8,9},{9,8},{10,11... | collective-permute-start | bytes 61448 | tf_op jit(solution)/shard_map/ppermute | solution.py:298
  32.2 5.0 %collective-permute-start.8 = (bf16[4,8,2048]{2,1,0:T(8,128)(2,1)S(1)}, bf16[4,8,2048]{2,1,0:T(8,128)(2,1)S(1)}, u32[]{:S(2)}, u32[]{:S(2)}) collective-permute-start(bf16[4,8,2048]{2,1,0:T(8,128)(2,1)S(1)} %get-tuple-element.30), channel_id=1, source_target_pairs={{0,1},{1,0},{2,3},{3,2},{4,5},{5,4},{6,7},{7,6},{8,9},{9,8},{10,11... | collective-permute-start | bytes 393224 | tf_op jit(solution)/shard_map/ppermute | solution.py:298
  33.4 3.9 %copy-start = (bf16[1,8,2048]{2,1,0:T(8,128)(2,1)S(1)}, bf16[1,8,2048]{2,1,0:T(8,128)(2,1)}, u32[]{:S(2)}) copy-start(bf16[1,8,2048]{2,1,0:T(8,128)(2,1)} %residual_ref.1) | copy-start | bytes 98308
  37.3 5.4 %collective-permute-start.11 = (bf16[2,8,2048]{2,1,0:T(8,128)(2,1)S(1)}, bf16[2,8,2048]{2,1,0:T(8,128)(2,1)S(1)}, u32[]{:S(2)}, u32[]{:S(2)}) collective-permute-start(bf16[2,8,2048]{2,1,0:T(8,128)(2,1)S(1)} %get-tuple-element.31), channel_id=1, source_target_pairs={{0,12},{1,13},{2,14},{3,15},{4,8},{5,9},{6,10},{7,11},{8,4},{9,5},... | collective-permute-start | bytes 196616 | tf_op jit(solution)/shard_map/ppermute | solution.py:298
  37.4 5.3 %collective-permute-start.9 = (bf16[2,8,2048]{2,1,0:T(8,128)(2,1)S(1)}, bf16[2,8,2048]{2,1,0:T(8,128)(2,1)S(1)}, u32[]{:S(2)}, u32[]{:S(2)}) collective-permute-start(bf16[2,8,2048]{2,1,0:T(8,128)(2,1)S(1)} %get-tuple-element.31), channel_id=1, source_target_pairs={{0,8},{1,9},{2,10},{3,11},{4,12},{5,13},{6,14},{7,15},{8,0},{9,1},... | collective-permute-start | bytes 196616 | tf_op jit(solution)/shard_map/ppermute | solution.py:298
  38.0 6.1 %collective-permute-start.12 = (bf16[2,8,2048]{2,1,0:T(8,128)(2,1)S(1)}, bf16[2,8,2048]{2,1,0:T(8,128)(2,1)S(1)}, u32[]{:S(2)}, u32[]{:S(2)}) collective-permute-start(bf16[2,8,2048]{2,1,0:T(8,128)(2,1)S(1)} %get-tuple-element.32), channel_id=1, source_target_pairs={{0,14},{1,15},{2,12},{3,13},{4,10},{5,11},{6,8},{7,9},{8,6},{9,7},... | collective-permute-start | bytes 196616 | tf_op jit(solution)/shard_map/ppermute | solution.py:298
  40.4 5.1 %collective-permute-start.10 = (bf16[2,8,2048]{2,1,0:T(8,128)(2,1)S(1)}, bf16[2,8,2048]{2,1,0:T(8,128)(2,1)S(1)}, u32[]{:S(2)}, u32[]{:S(2)}) collective-permute-start(bf16[2,8,2048]{2,1,0:T(8,128)(2,1)S(1)} %get-tuple-element.32), channel_id=1, source_target_pairs={{0,10},{1,11},{2,8},{3,9},{4,14},{5,15},{6,12},{7,13},{8,2},{9,3},... | collective-permute-start | bytes 196616 | tf_op jit(solution)/shard_map/ppermute | solution.py:298
  45.7 5.9 %collective-permute-start.15 = (bf16[2,8,2048]{2,1,0:T(8,128)(2,1)S(1)}, bf16[2,8,2048]{2,1,0:T(8,128)(2,1)S(1)}, u32[]{:S(2)}, u32[]{:S(2)}) collective-permute-start(bf16[2,8,2048]{2,1,0:T(8,128)(2,1)S(1)} %owner.1.refs_0_), channel_id=1, source_target_pairs={{0,3},{1,2},{2,1},{3,0},{4,7},{5,6},{6,5},{7,4},{8,11},{9,10},{10,... | collective-permute-start | bytes 196616 | tf_op jit(solution)/shard_map/ppermute | solution.py:298
  46.9 4.9 %collective-permute-start.14 = (bf16[2,8,2048]{2,1,0:T(8,128)(2,1)S(1)}, bf16[2,8,2048]{2,1,0:T(8,128)(2,1)S(1)}, u32[]{:S(2)}, u32[]{:S(2)}) collective-permute-start(bf16[2,8,2048]{2,1,0:T(8,128)(2,1)S(1)} %owner.1.refs_0_), channel_id=1, source_target_pairs={{0,2},{1,3},{2,0},{3,1},{4,6},{5,7},{6,4},{7,5},{8,10},{9,11},{10,... | collective-permute-start | bytes 196616 | tf_op jit(solution)/shard_map/ppermute | solution.py:298
  48.3 4.3 %collective-permute-start.13 = (bf16[2,8,2048]{2,1,0:T(8,128)(2,1)S(1)}, bf16[2,8,2048]{2,1,0:T(8,128)(2,1)S(1)}, u32[]{:S(2)}, u32[]{:S(2)}) collective-permute-start(bf16[2,8,2048]{2,1,0:T(8,128)(2,1)S(1)} %owner.1.refs_0_), channel_id=1, source_target_pairs={{0,1},{1,0},{2,3},{3,2},{4,5},{5,4},{6,7},{7,6},{8,9},{9,8},{10,11... | collective-permute-start | bytes 196616 | tf_op jit(solution)/shard_map/ppermute | solution.py:298
